TPU v7x, 256 devices: a whole 4x4x8 slice. The times are simulated.
256 devices in a mesh: sparse: 8 (over y, x_lo), rows: 32 (over z, x_hi, core).
Axes of the slice: x: 4 (x_hi: 2, x_lo: 2; x = x_hi * 2 + x_lo), y: 4, z: 8, core: 2. Of those that a mesh axis runs over, the one named last changes fastest.
Arguments:
- env_desc: bfloat16 [262144, 2048], P(('sparse', 'rows')), may hold values from -0.29882812 to 1
- sparse_desc: bfloat16 [2048, 2048], P('sparse'), may hold values from -0.29882812 to 1
- extra_atoms: int32 [8, 1024], P('sparse'), may hold values from 1 to 64, 17408 in all within a row
- owner_slots: int32 [8, 1024], P('sparse'), may hold values from 0 to 31, as said below
Outputs:
- energy_rows: float32 [8192, 2048], P(('sparse', 'rows'))
Inputs may be any that keep to these rules, and one draw needn't show every extreme that they name: Within each row of owner_slots, structures whose indices are equal modulo 32 have distinct values. The atoms of each row of extra_atoms fill exactly 1024 * 32 environments.
All inputs are finite; a program needn't handle non-finite values.
Results may differ from a plain program's by a relative error of at most 0.00087.
Values may be sent and summed in bfloat16 or wider, within the bound.
No kernel may reach another device: no remote copies, remote signals or barrier semaphores. Data moves between devices by JAX's collectives and lax.ppermute only.
A program may use at most 64 MiB of HBM per device.

v0:
```python
import jax
import jax.numpy as jnp
from jax import lax
from jax.sharding import PartitionSpec as P


def from_behind(array, axis, by):
    count = lax.axis_size(axis)
    return lax.ppermute(array, axis, [(i, (i + by) % count) for i in range(count)])


def unit_rows(desc):
    values = desc.astype(jnp.float32)
    return (values / jnp.sqrt(jnp.sum(values * values, axis=1, keepdims=True) + 1e-06)).astype(
        jnp.bfloat16
    )


def power_kernel(env_unit, block):
    inner = lax.dot_general(
        env_unit, block, (((1,), (1,)), ((), ())), preferred_element_type=jnp.float32
    )
    square = inner * inner
    return square * square


def on_device(env_desc, sparse_desc, extra_atoms, owner_slots):
    env_unit = unit_rows(env_desc)
    sparse_unit = unit_rows(sparse_desc)
    env_rows = env_desc.shape[0]
    block_cols = sparse_desc.shape[0]
    cycle_size = lax.axis_size("sparse")
    my_block = lax.axis_index("sparse")
    pieces = [(power_kernel(env_unit, sparse_unit), my_block)]
    moving = sparse_unit
    for step in range(1, cycle_size):
        moving = from_behind(moving, "sparse", 1)
        pieces.append((power_kernel(env_unit, moving), (my_block - step) % cycle_size))
    kernel = jnp.zeros((env_rows, block_cols * cycle_size), jnp.float32)
    for tile, where in pieces:
        kernel = lax.dynamic_update_slice_in_dim(kernel, tile, where * block_cols, 1)
    group_count = extra_atoms.shape[1]
    row_count = lax.axis_size("rows")
    my_row = lax.axis_index("rows")
    str_dev = group_count // row_count
    atom_min = env_rows // (2 * str_dev)
    local_count = 2 * str_dev + 2
    atoms = extra_atoms[0] + (atom_min - 1)
    slots = owner_slots[0]
    ends = jnp.cumsum(atoms)
    starts = ends - atoms
    base = my_row * env_rows
    first = jnp.sum((ends <= base).astype(jnp.int32))
    wanted = first + jnp.arange(local_count, dtype=jnp.int32)
    select = (jnp.arange(group_count, dtype=jnp.int32)[None, :] == wanted[:, None]).astype(
        jnp.int32
    )
    local_start = jnp.sum(select * starts[None, :], axis=1)
    local_end = jnp.sum(select * ends[None, :], axis=1)
    local_slot = jnp.sum(select * slots[None, :], axis=1)
    present = jnp.sum(select, axis=1) > 0
    position = base + jnp.arange(env_rows, dtype=jnp.int32)
    member = (
        (position[None, :] >= local_start[:, None]) & (position[None, :] < local_end[:, None])
    ).astype(jnp.float32)
    partial_sums = jnp.dot(
        member, kernel, precision=lax.Precision.HIGH, preferred_element_type=jnp.float32
    )
    local_row = wanted % row_count * str_dev + local_slot
    targets = jnp.arange(str_dev * lax.axis_size("rows"), dtype=jnp.int32)
    pick = ((local_row[None, :] == targets[:, None]) & present[None, :]).astype(jnp.float32)
    summed = lax.psum_scatter(
        jnp.dot(
            pick, partial_sums, precision=lax.Precision.HIGH, preferred_element_type=jnp.float32
        ),
        "rows",
        scatter_dimension=0,
        tiled=True,
    )
    structure = jnp.arange(group_count, dtype=jnp.int32)
    mine = structure % row_count == my_row
    owned = jnp.arange(str_dev, dtype=jnp.int32)
    match = ((slots[None, :] == owned[:, None]) & mine[None, :]).astype(jnp.int32)
    owned_atoms = jnp.sum(match * atoms[None, :], axis=1)
    return summed / owned_atoms.astype(jnp.float32)[:, None]


def solution(mesh):
    placed = (P(("sparse", "rows"), None), P("sparse", None), P("sparse", None), P("sparse", None))
    return jax.shard_map(
        on_device,
        mesh=mesh,
        in_specs=placed,
        out_specs=P(("sparse", "rows"), None),
        check_vma=False,
    )
```

profile of v0, /device:TPU:6, one launch (start us, length us, event | category | flops | bytes accessed | tf_op | source)
XLA Modules:
  0.0 351.9 jit_solution(17340665545938122401)
XLA Ops:
  6.5 0.0 reduce-scatter.2.cloned.1.call-start
  6.5 1.5 fusion.2
  8.1 1.6 fusion.3
  9.7 1.9 collective-permute-start
  11.6 23.1 %collective-permute-done = bf16[256,2048]{1,0:T(8,128)(2,1)S(1)} collective-permute-done((bf16[256,2048]{1,0:T(8,128)(2,1)S(1)}, bf16[256,2048]{1,0:T(8,128)(2,1)S(1)}, u32[]{:S(2)}, u32[]{:S(2)}) %collective-permute-start) | collective-permute-done | bytes 1048608 | tf_op jit(solution)/shard_map/ppermute | solution.py:9
  34.6 2.7 collective-permute-start.1
  37.4 22.5 %collective-permute-done.1 = bf16[256,2048]{1,0:T(8,128)(2,1)S(1)} collective-permute-done((bf16[256,2048]{1,0:T(8,128)(2,1)S(1)}, bf16[256,2048]{1,0:T(8,128)(2,1)S(1)}, u32[]{:S(2)}, u32[]{:S(2)}) %collective-permute-start.1) | collective-permute-done | bytes 1048608 | tf_op jit(solution)/shard_map/ppermute | solution.py:9
  59.9 2.4 collective-permute-start.2
  62.3 0.7 broadcast_add_fusion.1
  63.0 0.3 reduce-window.9
  63.3 0.1 slice.7
  63.4 0.1 slice_reduce_fusion
  63.5 0.7 convert_reduce_fusion.1
  64.2 0.6 iota_add_fusion.1
  64.9 0.7 fusion.40
  65.6 1.0 convert_reduce_fusion
  66.5 18.6 %collective-permute-done.2 = bf16[256,2048]{1,0:T(8,128)(2,1)} collective-permute-done((bf16[256,2048]{1,0:T(8,128)(2,1)S(1)}, bf16[256,2048]{1,0:T(8,128)(2,1)}, u32[]{:S(2)}, u32[]{:S(2)}) %collective-permute-start.2) | collective-permute-done | bytes 1048608 | tf_op jit(solution)/shard_map/ppermute | solution.py:9
  85.2 1.2 collective-permute-start.3
  86.4 0.7 fusion.38
  87.1 3.1 fusion
  90.2 19.6 %collective-permute-done.3 = bf16[256,2048]{1,0:T(8,128)(2,1)} collective-permute-done((bf16[256,2048]{1,0:T(8,128)(2,1)}, bf16[256,2048]{1,0:T(8,128)(2,1)}, u32[]{:S(2)}, u32[]{:S(2)}) %collective-permute-start.3) | collective-permute-done | bytes 1048608 | tf_op jit(solution)/shard_map/ppermute | solution.py:9
  109.8 0.0 collective-permute-start.4
  109.8 3.9 %fusion.1 = bf16[1024,2048]{1,0:T(8,128)(2,1)S(1)} fusion(bf16[1024,2048]{1,0:T(8,128)(2,1)} %param.4, f32[1024]{0:T(1024)S(1)} %add_sqrt_fusion), kind=kLoop, calls=%fused_computation.3 | loop fusion | flops 6291456 | bytes 8392704 | tf_op jit(solution)/shard_map/convert_element_type | solution.py:14
  113.8 1.0 broadcast_in_dim.2
  114.8 1.3 fusion.19
  116.1 17.3 %collective-permute-done.4 = bf16[256,2048]{1,0:T(8,128)(2,1)S(1)} collective-permute-done((bf16[256,2048]{1,0:T(8,128)(2,1)}, bf16[256,2048]{1,0:T(8,128)(2,1)S(1)}, u32[]{:S(2)}, u32[]{:S(2)}) %collective-permute-start.4) | collective-permute-done | bytes 1048608 | tf_op jit(solution)/shard_map/ppermute | solution.py:9
  133.4 0.0 collective-permute-start.5
  133.4 1.3 fusion.17
  134.7 1.3 fusion.15
  136.0 2.5 fusion.13
  138.5 18.2 %collective-permute-done.5 = bf16[256,2048]{1,0:T(8,128)(2,1)S(1)} collective-permute-done((bf16[256,2048]{1,0:T(8,128)(2,1)S(1)}, bf16[256,2048]{1,0:T(8,128)(2,1)S(1)}, u32[]{:S(2)}, u32[]{:S(2)}) %collective-permute-start.5) | collective-permute-done | bytes 1048608 | tf_op jit(solution)/shard_map/ppermute | solution.py:9
  156.7 0.0 collective-permute-start.6
  156.7 2.5 fusion.11
  159.2 1.3 fusion.9
  160.5 1.3 fusion.7
  161.8 16.5 %collective-permute-done.6 = bf16[256,2048]{1,0:T(8,128)(2,1)S(1)} collective-permute-done((bf16[256,2048]{1,0:T(8,128)(2,1)S(1)}, bf16[256,2048]{1,0:T(8,128)(2,1)S(1)}, u32[]{:S(2)}, u32[]{:S(2)}) %collective-permute-start.6) | collective-permute-done | bytes 1048608 | tf_op jit(solution)/shard_map/ppermute | solution.py:9
  178.3 1.3 fusion.5
  179.7 2.0 fusion.23
  181.7 0.0 copy-start
  181.7 5.6 %fusion.21 = f32[1024,2048]{1,0:T(8,128)} fusion(f32[66,2048]{1,0:T(8,128)S(1)} %fusion.23, s32[66]{0:T(128)S(1)} %fusion.38, pred[66]{0:T(512)(128)(4,1)S(1)} %broadcast_compare_fusion), kind=kOutput, calls=%fused_computation.34 | convolution fusion | flops 830607360 | bytes 8929610 | tf_op jit(solution)/shard_map/dot_general | solution.py:73
  187.2 0.0 reduce-scatter.2.cloned.1.call-update
  187.3 0.0 copy-done
  187.3 0.1 select_reduce_fusion.3
  187.4 155.9 %reduce-scatter.2.cloned.1.call-done = f32[32,2048]{1,0:T(8,128)} async-done(((f32[1024,2048]{1,0:T(8,128)}), f32[32,2048]{1,0:T(8,128)}) %reduce-scatter.2.cloned.1.call-update) | async-done | bytes 262160 | tf_op jit(solution)/shard_map/reduce_scatter | solution.py:72
  343.3 1.7 broadcast_divide_fusion
  (7 shorter events, 0.1 us)
Async XLA Ops:
  6.5 336.8 %reduce-scatter.2.cloned.1.call-start = ((), (), s32[]{:S(2)}) async-start(), calls=%async_computation.1 | async-start | bytes 8650752 | tf_op jit(solution)/shard_map/reduce_scatter | solution.py:72
  9.7 25.0 %collective-permute-start = (bf16[256,2048]{1,0:T(8,128)(2,1)S(1)}, bf16[256,2048]{1,0:T(8,128)(2,1)S(1)}, u32[]{:S(2)}, u32[]{:S(2)}) collective-permute-start(bf16[256,2048]{1,0:T(8,128)(2,1)S(1)} %fusion.3), channel_id=1, source_target_pairs={{0,32},{32,64},{64,96},{96,128},{128,160},{160,192},{192,224},{224... | collective-permute-start | bytes 3145736 | tf_op jit(solution)/shard_map/ppermute | solution.py:9
  34.6 25.2 %collective-permute-start.1 = (bf16[256,2048]{1,0:T(8,128)(2,1)S(1)}, bf16[256,2048]{1,0:T(8,128)(2,1)S(1)}, u32[]{:S(2)}, u32[]{:S(2)}) collective-permute-start(bf16[256,2048]{1,0:T(8,128)(2,1)S(1)} %collective-permute-done), channel_id=1, source_target_pairs={{0,32},{32,64},{64,96},{96,128},{128,160},{160,192},{192,224},{224... | collective-permute-start | bytes 3145736 | tf_op jit(solution)/shard_map/ppermute | solution.py:9
  59.9 25.3 %collective-permute-start.2 = (bf16[256,2048]{1,0:T(8,128)(2,1)S(1)}, bf16[256,2048]{1,0:T(8,128)(2,1)}, u32[]{:S(2)}, u32[]{:S(2)}) collective-permute-start(bf16[256,2048]{1,0:T(8,128)(2,1)S(1)} %collective-permute-done.1), channel_id=1, source_target_pairs={{0,32},{32,64},{64,96},{96,128},{128,160},{160,192},{192,224},{224... | collective-permute-start | bytes 3145736 | tf_op jit(solution)/shard_map/ppermute | solution.py:9
  85.2 24.6 %collective-permute-start.3 = (bf16[256,2048]{1,0:T(8,128)(2,1)}, bf16[256,2048]{1,0:T(8,128)(2,1)}, u32[]{:S(2)}, u32[]{:S(2)}) collective-permute-start(bf16[256,2048]{1,0:T(8,128)(2,1)} %collective-permute-done.2), channel_id=1, source_target_pairs={{0,32},{32,64},{64,96},{96,128},{128,160},{160,192},{192,224},{224... | collective-permute-start | bytes 3145736 | tf_op jit(solution)/shard_map/ppermute | solution.py:9
  109.8 23.6 %collective-permute-start.4 = (bf16[256,2048]{1,0:T(8,128)(2,1)}, bf16[256,2048]{1,0:T(8,128)(2,1)S(1)}, u32[]{:S(2)}, u32[]{:S(2)}) collective-permute-start(bf16[256,2048]{1,0:T(8,128)(2,1)} %collective-permute-done.3), channel_id=1, source_target_pairs={{0,32},{32,64},{64,96},{96,128},{128,160},{160,192},{192,224},{224... | collective-permute-start | bytes 3145736 | tf_op jit(solution)/shard_map/ppermute | solution.py:9
  133.4 23.3 %collective-permute-start.5 = (bf16[256,2048]{1,0:T(8,128)(2,1)S(1)}, bf16[256,2048]{1,0:T(8,128)(2,1)S(1)}, u32[]{:S(2)}, u32[]{:S(2)}) collective-permute-start(bf16[256,2048]{1,0:T(8,128)(2,1)S(1)} %collective-permute-done.4), channel_id=1, source_target_pairs={{0,32},{32,64},{64,96},{96,128},{128,160},{160,192},{192,224},{224... | collective-permute-start | bytes 3145736 | tf_op jit(solution)/shard_map/ppermute | solution.py:9
  156.7 21.6 %collective-permute-start.6 = (bf16[256,2048]{1,0:T(8,128)(2,1)S(1)}, bf16[256,2048]{1,0:T(8,128)(2,1)S(1)}, u32[]{:S(2)}, u32[]{:S(2)}) collective-permute-start(bf16[256,2048]{1,0:T(8,128)(2,1)S(1)} %collective-permute-done.5), channel_id=1, source_target_pairs={{0,32},{32,64},{64,96},{96,128},{128,160},{160,192},{192,224},{224... | collective-permute-start | bytes 3145736 | tf_op jit(solution)/shard_map/ppermute | solution.py:9
  181.7 5.6 %copy-start = (s32[1,1024]{1,0:T(1,128)S(1)}, s32[1,1024]{1,0:T(1,128)}, u32[]{:S(2)}) copy-start(s32[1,1024]{1,0:T(1,128)} %param.7) | copy-start | bytes 12292
Sparse Core Ops, SparseCore 0:
  187.4 155.9 reduce-scatter.1
where the time goes:
time: 354 us; the launch traced here: 352 us
  waiting for transfers between devices  292 us (82%)
  matrix products  20.4 us (6%)
  other arithmetic  16.7 us (5%)
  between operations  13.5 us (4%)
  starting transfers between devices  8.37 us (2%)
    reduce_scatter x1, waiting for transfers between devices, on_device(): lax.psum_scatter(jnp.dot(pick, partial_sums, precision=lax.Precision.HIGH...  156 us
    ppermute x7, waiting for transfers between devices, from_behind(): lax.ppermute(array, axis, [(i, (i + by) % count) for i in range(count)])  136 us
    dot_general x8, matrix products, power_kernel(): lax.dot_general(env_unit, block, (((1,), (1,)), ((), ())), preferred_elem...  12.9 us
    ppermute x7, starting transfers between devices, from_behind(): lax.ppermute(array, axis, [(i, (i + by) % count) for i in range(count)])  8.37 us
  transfers between devices with their start and end apart: 8, of which 8 were waited for; matrix products, arithmetic and copies ran while one was open for 7% of the time, Pallas kernels for 0%

commit v1 on v0

v1 whole, which is shorter than its diff:
```python
import jax
import jax.numpy as jnp
from jax import lax
from jax.experimental import pallas as pl
from jax.experimental.pallas import tpu as pltpu
from jax.sharding import PartitionSpec as P

Y, XL, Z, XH, CORE = 4, 2, 8, 2, 2
CHIPS = Z * XH
ROWS = CHIPS * CORE
HALO = 16
KEEP = 4
MIB = 1 << 20


def move(array, to):
    pairs = []
    for y in range(Y):
        for xl in range(XL):
            for z in range(Z):
                for xh in range(XH):
                    for core in range(CORE):
                        target = to(y, xl, z, xh, core)
                        if target is not None:
                            pairs.append((place(y, xl, z, xh, core), place(*target)))
    return lax.ppermute(array, ("sparse", "rows"), pairs)


def place(y, xl, z, xh, core):
    return (((y % Y * XL + xl) * Z + z % Z) * XH + xh) * CORE + core


def up(y, xl, z, xh, core):
    return y + 1, xl, z, xh, core


def down(y, xl, z, xh, core):
    return y - 1, xl, z, xh, core


def across(y, xl, z, xh, core):
    return y, 1 - xl, z, xh, core


def around(y, xl, z, xh, core):
    return y, 1 - xl, z, (xh + 1) % XH, core


def other_core(y, xl, z, xh, core):
    return y, xl, z, xh, 1 - core


def next_chip(to_core):
    def to(y, xl, z, xh, core):
        if core == 0:
            return None
        return y, xl, (z if xh == 0 else z + 1), 1 - xh, to_core

    return to


def unit(desc):
    values = desc.astype(jnp.float32)
    scale = 1.0 / jnp.sqrt(jnp.sum(values * values, axis=1, keepdims=True) + 1e-06)
    return (values * scale).astype(jnp.bfloat16)


def sparse_unit_kernel(core_ref, desc_ref, a_ref, b_ref):
    quarter = a_ref.shape[0]
    at = pl.multiple_of(core_ref[0] * (2 * quarter), 2 * quarter)
    a_ref[...] = unit(desc_ref[pl.ds(at, quarter), :])
    b_ref[...] = unit(desc_ref[pl.ds(at + quarter, quarter), :])


def sparse_unit(core, desc):
    rows, width = desc.shape
    piece = jax.ShapeDtypeStruct((rows // 4, width), jnp.bfloat16)
    return pl.pallas_call(
        sparse_unit_kernel,
        in_specs=[
            pl.BlockSpec(memory_space=pltpu.SMEM),
            pl.BlockSpec(memory_space=pltpu.VMEM),
        ],
        out_specs=[pl.BlockSpec(memory_space=pltpu.VMEM)] * 2,
        out_shape=[piece, piece],
        compiler_params=pltpu.CompilerParams(vmem_limit_bytes=16 * MIB),
        cost_estimate=pl.CostEstimate(
            flops=4 * rows * width, bytes_accessed=4 * rows * width, transcendentals=rows
        ),
    )(core, desc)


def env_unit_kernel(desc_ref, out_ref):
    out_ref[...] = unit(desc_ref[...])


def env_unit(desc):
    rows, width = desc.shape
    tile = 128
    return pl.pallas_call(
        env_unit_kernel,
        grid=(rows // tile,),
        in_specs=[pl.BlockSpec((tile, width), lambda i: (i, 0))],
        out_specs=pl.BlockSpec((tile, width), lambda i: (i, 0)),
        out_shape=jax.ShapeDtypeStruct((rows, width), jnp.bfloat16),
        compiler_params=pltpu.CompilerParams(vmem_limit_bytes=16 * MIB),
        cost_estimate=pl.CostEstimate(
            flops=6 * rows * width, bytes_accessed=4 * rows * width, transcendentals=rows
        ),
    )(desc)


def power_sums(env, block, member):
    inner = lax.dot_general(env, block, (((1,), (1,)), ((), ())), preferred_element_type=jnp.float32)
    square = inner * inner
    kernel = square * square
    high = kernel.astype(jnp.bfloat16)
    low = (kernel - high.astype(jnp.float32)).astype(jnp.bfloat16)
    return jnp.dot(member, high, preferred_element_type=jnp.float32) + jnp.dot(
        member, low, preferred_element_type=jnp.float32
    )


def main_kernel(
    p0, p1, p2, p3, own, other, halo, of_own, of_other, of_halo, out_ref, block, total
):
    step = pl.program_id(0)

    @pl.when(step == 0)
    def _():
        quarter = p0.shape[0]
        for i, piece in enumerate((p0, p1, p2, p3)):
            block[i * quarter : (i + 1) * quarter, :] = piece[...]
        total[...] = power_sums(unit(halo[...]), block[...], of_halo[...])

    total[...] += power_sums(own[...], block[...], of_own[...])
    total[...] += power_sums(other[...], block[...], of_other[...])

    @pl.when(step == pl.num_programs(0) - 1)
    def _():
        sums = total[...].reshape(ROWS // 2, 2 * KEEP, 256)
        left, right = sums[:, :, :128], sums[:, :, 128:]
        lower = lax.broadcasted_iota(jnp.int32, left.shape, 1) < KEEP
        out_ref[:, 0] = jnp.where(lower, left, jnp.roll(right, KEEP, axis=1))
        out_ref[:, 1] = jnp.where(lower, jnp.roll(left, KEEP, axis=1), right)


def main(pieces, own, other, halo, members):
    rows, width = own.shape
    tile = 256
    quarter = pieces[0].shape[0]
    columns = 4 * quarter
    of_own, of_other, of_halo = members
    count = of_own.shape[0]
    whole = lambda i: (0, 0)
    return pl.pallas_call(
        main_kernel,
        grid=(rows // tile,),
        in_specs=[pl.BlockSpec((quarter, width), whole)] * 4
        + [pl.BlockSpec((tile, width), lambda i: (i, 0))] * 2
        + [pl.BlockSpec((HALO, width), whole)]
        + [pl.BlockSpec((count, tile), lambda i: (0, i))] * 2
        + [pl.BlockSpec((count, HALO), whole)],
        out_specs=pl.BlockSpec((ROWS // 2, 2, 2 * KEEP, 128), lambda i: (0, 0, 0, 0)),
        out_shape=jax.ShapeDtypeStruct((ROWS // 2, 2, 2 * KEEP, 128), jnp.float32),
        scratch_shapes=[
            pltpu.VMEM((columns, width), jnp.bfloat16),
            pltpu.VMEM((count, columns), jnp.float32),
        ],
        compiler_params=pltpu.CompilerParams(vmem_limit_bytes=32 * MIB),
        cost_estimate=pl.CostEstimate(
            flops=4 * rows * width * columns, bytes_accessed=4 * rows * width, transcendentals=0
        ),
    )(*pieces, own, other, halo, of_own, of_other, of_halo)


def combine_kernel(column_ref, got_ref, pick_ref, atoms_ref, out_ref):
    pick = pick_ref[...]
    count = pick.shape[0] // 2
    for core in range(CORE):
        for call in range(4):
            rows = got_ref[:, core, 8 * call : 8 * (call + 1), :].reshape(8 * CHIPS, 128)
            high = rows.astype(jnp.bfloat16)
            rest = rows - high.astype(jnp.float32)
            mid = rest.astype(jnp.bfloat16)
            low = (rest - mid.astype(jnp.float32)).astype(jnp.bfloat16)
            sums = (
                jnp.dot(pick, low, preferred_element_type=jnp.float32)
                + jnp.dot(pick, mid, preferred_element_type=jnp.float32)
                + jnp.dot(pick, high, preferred_element_type=jnp.float32)
            )
            for half in range(2):
                at = pl.multiple_of(column_ref[(core * 4 + call) * 2 + half] * 128, 128)
                out_ref[:, pl.ds(at, 128)] = sums[half * count : (half + 1) * count] / atoms_ref[...]


def combine(columns, got, pick, atoms, width):
    count = pick.shape[0] // 2
    return pl.pallas_call(
        combine_kernel,
        in_specs=[pl.BlockSpec(memory_space=pltpu.SMEM)]
        + [pl.BlockSpec(memory_space=pltpu.VMEM)] * 3,
        out_specs=pl.BlockSpec(memory_space=pltpu.VMEM),
        out_shape=jax.ShapeDtypeStruct((count, width), jnp.float32),
        compiler_params=pltpu.CompilerParams(vmem_limit_bytes=16 * MIB),
    )(columns, got, pick, atoms)


def on_device(env_desc, sparse_desc, extra_atoms, owner_slots):
    env_rows, _ = env_desc.shape
    block_cols = sparse_desc.shape[0]
    groups = extra_atoms.shape[1]
    str_dev = groups // ROWS
    atom_min = env_rows // (2 * str_dev)
    my_block, my_row = lax.axis_index("sparse"), lax.axis_index("rows")
    y, xl = my_block // XL, my_block % XL
    chip, core = my_row // CORE, my_row % CORE

    a, b = sparse_unit(core.reshape(1).astype(jnp.int32), sparse_desc)
    up_a, down_b = move(a, up), move(b, down)
    near_a, near_b = move(a, across), move(b, around)
    up_b, down_a = move(b, up), move(a, down)
    own = env_unit(env_desc)
    tail = env_desc[env_rows - HALO :]
    halo = jnp.where(core == 0, move(tail, next_chip(0)), move(tail, next_chip(1)))
    other = move(own, other_core)
    far_a, far_b = move(up_a, up), move(down_b, down)
    near_up_a, near_down_b = move(up_a, across), move(down_b, around)
    near_up_b, near_down_a = move(up_b, around), move(down_a, across)
    near_far_a, near_far_b = move(far_a, across), move(far_b, around)

    atoms = extra_atoms[0] + (atom_min - 1)
    slots = owner_slots[0]
    ends = jnp.cumsum(atoms)
    starts = ends - atoms
    chip_rows = CORE * env_rows
    bases = jnp.arange(CHIPS, dtype=jnp.int32) * chip_rows
    firsts = jnp.sum((ends[None, :] <= bases[:, None]).astype(jnp.int32), axis=1)
    chips = jnp.arange(CHIPS, dtype=jnp.int32)
    first = jnp.sum(jnp.where(chips == chip, firsts, 0))
    before = jnp.sum(jnp.where(chips == chip - 1, firsts, 0))
    base = chip * chip_rows
    spilled = (chip > 0) & (first - before == ROWS * KEEP)
    owners = jnp.arange(ROWS, dtype=jnp.int32)[:, None]
    keeps = jnp.arange(KEEP, dtype=jnp.int32)[None, :]
    held = (first + (owners - first) % ROWS + ROWS * keeps).reshape(-1)
    structure = jnp.arange(groups, dtype=jnp.int32)
    select = (structure[None, :] == held[:, None]).astype(jnp.int32)
    held_start = jnp.sum(select * starts[None, :], axis=1)
    held_end = jnp.sum(select * ends[None, :], axis=1)
    lower = jnp.maximum(held_start, jnp.where(spilled, base - HALO, base))[:, None]
    upper = held_end[:, None]

    def member(begin, count):
        position = begin + jnp.arange(count, dtype=jnp.int32)[None, :]
        return ((position >= lower) & (position < upper)).astype(jnp.bfloat16)

    members = (
        member(base + core * env_rows, env_rows),
        member(base + (1 - core) * env_rows, env_rows),
        member(base - HALO, HALO),
    )

    sent = firsts[:, None] + (my_row - firsts[:, None]) % ROWS + ROWS * keeps
    select = (structure[None, :] == sent.reshape(-1)[:, None]).astype(jnp.int32)
    slot = jnp.sum(select * (slots[None, :] + 1), axis=1).reshape(1, 1, CHIPS, 1, KEEP) - 1
    rows = jnp.arange(str_dev, dtype=jnp.int32).reshape(1, str_dev, 1, 1, 1)
    half = jnp.arange(2, dtype=jnp.int32)
    same = half.reshape(2, 1, 1, 1, 1) == half.reshape(1, 1, 1, 2, 1)
    pick = ((slot == rows) & same).astype(jnp.bfloat16).reshape(2 * str_dev, CHIPS * 2 * KEEP)
    mine = structure % ROWS == my_row
    owned = jnp.arange(str_dev, dtype=jnp.int32)
    match = ((slots[None, :] == owned[:, None]) & mine[None, :]).astype(jnp.int32)
    owned_atoms = jnp.sum(match * atoms[None, :], axis=1).astype(jnp.float32)[:, None]
    shifts = jnp.array([[0, 0], [0, 1], [3, 0], [1, 0], [3, 1], [1, 1], [2, 0], [2, 1]], jnp.int32)
    blocks = (y + shifts[:, 0]) % Y * XL + (xl + shifts[:, 1]) % XL
    columns = (blocks[None, :] * 2 + jnp.arange(CORE, dtype=jnp.int32)[:, None]).reshape(-1)

    sums = [
        main(pieces, own, other, halo, members)
        for pieces in (
            (a, b, near_a, near_b),
            (up_a, up_b, down_a, down_b),
            (near_up_a, near_up_b, near_down_a, near_down_b),
            (far_a, far_b, near_far_a, near_far_b),
        )
    ]
    partial_sums = jnp.concatenate(sums, axis=2).reshape(ROWS, 8 * 4, 128)
    got = lax.all_to_all(partial_sums, "rows", 0, 0, tiled=True)
    return combine(
        columns.astype(jnp.int32),
        got.reshape(CHIPS, CORE, 8 * 4, 128),
        pick,
        owned_atoms,
        block_cols * Y * XL,
    )


def solution(mesh):
    placed = (P(("sparse", "rows"), None), P("sparse", None), P("sparse", None), P("sparse", None))
    return jax.shard_map(
        on_device,
        mesh=mesh,
        in_specs=placed,
        out_specs=P(("sparse", "rows"), None),
        check_vma=False,
    )
```

time: 354 us -> 117 us (0.33)
  waiting for transfers between devices: 292 us -> 29 us
  Pallas kernels: 0 us -> 41.6 us
  starting transfers between devices: 8.37 us -> 35.5 us
  matrix products: 20.4 us -> 0 us
  other arithmetic: 16.7 us -> 4.06 us
  between operations: 13.5 us -> 1.59 us
  local copies, waits for them, and re-layouts: 1.23 us -> 5.09 us
    reduce_scatter x1 -> x0, waiting for transfers between devices: 156 us -> none  [on_device(): lax.psum_scatter(jnp.dot(pick, partial_sums, precision=lax.Precision.HIGH...]
    ppermute x7 -> x17, waiting for transfers between devices: 136 us -> 12 us  [move(): return lax.ppermute(array, ('sparse', 'rows'), pairs)]
    pallas_call x0 -> x7, Pallas kernels: none -> 41.6 us  [the longest x4 35.5 us: main(): pl.pallas_call(main_kernel, grid=(rows // tile,), in_specs=[pl.BlockSpec(...]
    dot_general x10 -> x0, matrix products: 20.4 us -> none  [the longest x8 12.9 us: power_kernel(): lax.dot_general(env_unit, block, (((1,), (1,)), ((), ())), preferred_elem...]
    all_to_all x0 -> x1, waiting for transfers between devices: none -> 17 us  [on_device(): got = lax.all_to_all(partial_sums, 'rows', 0, 0, tiled=True)]
    ppermute x7 -> x17, starting transfers between devices: 8.37 us -> 24.8 us  [move(): return lax.ppermute(array, ('sparse', 'rows'), pairs)]
    all_to_all x0 -> x1, starting transfers between devices: none -> 10.7 us  [on_device(): got = lax.all_to_all(partial_sums, 'rows', 0, 0, tiled=True)]
    convert_element_type x3 -> x4, other arithmetic: 5.55 us -> 0.46 us  [the longest x2 0.32 us: member(): return ((position >= lower) & (position < upper)).astype(jnp.bfloat16)]
  transfers between devices with their start and end apart: 8 -> 18, of which waited for: 8 -> 4; matrix products, arithmetic and copies ran while one was open for 7% -> 3% of each run, Pallas kernels for 0% -> 27%
where the time goes in v1:
time: 117 us
  Pallas kernels  41.6 us (36%)
  starting transfers between devices  35.5 us (30%)
  waiting for transfers between devices  29 us (25%)
  local copies, waits for them, and re-layouts  5.09 us (4%)
  other arithmetic  4.06 us (3%)
  between operations  1.59 us (1%)
    pallas_call x4, Pallas kernels, main(): pl.pallas_call(main_kernel, grid=(rows // tile,), in_specs=[pl.BlockSpec(...  35.5 us
    ppermute x17, starting transfers between devices, move(): return lax.ppermute(array, ('sparse', 'rows'), pairs)  24.8 us
    all_to_all x1, waiting for transfers between devices, on_device(): got = lax.all_to_all(partial_sums, 'rows', 0, 0, tiled=True)  17 us
    ppermute x17, waiting for transfers between devices, move(): return lax.ppermute(array, ('sparse', 'rows'), pairs)  12 us
    all_to_all x1, starting transfers between devices, on_device(): got = lax.all_to_all(partial_sums, 'rows', 0, 0, tiled=True)  10.7 us
    pallas_call x1, Pallas kernels, env_unit(): pl.pallas_call(env_unit_kernel, grid=(rows // tile,), in_specs=[pl.BlockS...  4.31 us
    unnamed x12, local copies, waits for them, and re-layouts  3.43 us
  transfers between devices with their start and end apart: 18, of which 4 were waited for; matrix products, arithmetic and copies ran while one was open for 3% of the time, Pallas kernels for 27%

profile of v1, /device:TPU:6, one launch (start us, length us, event | category | flops | bytes accessed | tf_op | source)
XLA Modules:
  0.0 116.8 jit_solution(2955027454670912645)
XLA Ops:
  0.0 0.8 slice.18
  0.8 1.3 %collective-permute-start.3 = (bf16[16,2048]{1,0:T(8,128)(2,1)S(1)}, bf16[16,2048]{1,0:T(8,128)(2,1)S(1)}, u32[]{:S(2)}, u32[]{:S(2)}) collective-permute-start(bf16[16,2048]{1,0:T(8,128)(2,1)S(1)} %slice.18), channel_id=1, source_target_pairs={{1,2},{3,4},{5,6},{7,8},{9,10},{11,12},{13,14},{15,16},{17,18},{19... | collective-permute-start | bytes 196616 | tf_op jit(solution)/shard_map/ppermute | solution.py:26
  2.1 0.7 collective-permute-start.4
  2.8 1.2 %copy-done.1 = bf16[256,2048]{1,0:T(8,128)(2,1)S(1)} copy-done((bf16[256,2048]{1,0:T(8,128)(2,1)S(1)}, bf16[256,2048]{1,0:T(8,128)(2,1)}, u32[]{:S(2)}) %copy-start.1) | copy-done | bytes 1048600
  4.0 0.2 shard_map.55
  4.3 1.7 %collective-permute-start.5 = (bf16[64,2048]{1,0:T(8,128)(2,1)S(1)}, bf16[64,2048]{1,0:T(8,128)(2,1)S(1)}, u32[]{:S(2)}, u32[]{:S(2)}) collective-permute-start(bf16[64,2048]{1,0:T(8,128)(2,1)S(1)} %get-tuple-element.7.p0), channel_id=1, source_target_pairs={{0,64},{1,65},{2,66},{3,67},{4,68},{5,69},{6,70},{7,71},{8,72},{9,... | collective-permute-start | bytes 786440 | tf_op jit(solution)/shard_map/ppermute | solution.py:26
  5.9 1.7 %collective-permute-start.7 = (bf16[64,2048]{1,0:T(8,128)(2,1)S(1)}, bf16[64,2048]{1,0:T(8,128)(2,1)S(1)}, u32[]{:S(2)}, u32[]{:S(2)}) collective-permute-start(bf16[64,2048]{1,0:T(8,128)(2,1)S(1)} %get-tuple-element.7.p0), channel_id=1, source_target_pairs={{0,192},{1,193},{2,194},{3,195},{4,196},{5,197},{6,198},{7,199},{8... | collective-permute-start | bytes 786440 | tf_op jit(solution)/shard_map/ppermute | solution.py:26
  7.6 2.2 %copy-done = bf16[1024,2048]{1,0:T(8,128)(2,1)S(1)} copy-done((bf16[1024,2048]{1,0:T(8,128)(2,1)S(1)}, bf16[1024,2048]{1,0:T(8,128)(2,1)}, u32[]{:S(2)}) %copy-start) | copy-done | bytes 4194328
  9.8 4.3 %shard_map.56.own = bf16[1024,2048]{1,0:T(8,128)(2,1)} custom-call(bf16[1024,2048]{1,0:T(8,128)(2,1)S(1)} %copy-done), custom_call_target="tpu_custom_call" | custom-call | flops 12582912 | bytes 8388608 | tf_op jit(solution)/shard_map/pallas_call | solution.py:100
  14.1 6.2 %collective-permute-start.2 = (bf16[1024,2048]{1,0:T(8,128)(2,1)}, bf16[1024,2048]{1,0:T(8,128)(2,1)}, u32[]{:S(2)}, u32[]{:S(2)}) collective-permute-start(bf16[1024,2048]{1,0:T(8,128)(2,1)} %shard_map.56.own), channel_id=1, source_target_pairs={{0,1},{1,0},{2,3},{3,2},{4,5},{5,4},{6,7},{7,6},{8,9},{9,8},{10,11... | collective-permute-start | bytes 12582920 | tf_op jit(solution)/shard_map/ppermute | solution.py:26
  20.3 0.3 reduce-window.9
  20.6 0.1 slice_reduce_fusion
  20.8 0.2 convert_reduce_fusion
  21.0 0.7 fusion.10
  22.9 0.6 fusion.9
  23.6 0.1 add.261
  23.7 0.1 add.272
  23.9 0.2 select_reduce_fusion.2
  24.2 0.2 select_reduce_fusion.1
  24.5 0.1 and_convert_fusion.3.of_halo
  24.7 0.3 collective-permute-start.6
  25.0 3.0 %collective-permute-start.8 = (bf16[64,2048]{1,0:T(8,128)(2,1)S(1)}, bf16[64,2048]{1,0:T(8,128)(2,1)S(1)}, u32[]{:S(2)}, u32[]{:S(2)}) collective-permute-start(bf16[64,2048]{1,0:T(8,128)(2,1)S(1)} %get-tuple-element.8.p1), channel_id=1, source_target_pairs={{0,192},{1,193},{2,194},{3,195},{4,196},{5,197},{6,198},{7,199},{8... | collective-permute-start | bytes 786440 | tf_op jit(solution)/shard_map/ppermute | solution.py:26
  28.1 0.2 and_convert_fusion
  28.3 6.9 %collective-permute-done.6.p1 = bf16[64,2048]{1,0:T(8,128)(2,1)S(1)} collective-permute-done((bf16[64,2048]{1,0:T(8,128)(2,1)S(1)}, bf16[64,2048]{1,0:T(8,128)(2,1)S(1)}, u32[]{:S(2)}, u32[]{:S(2)}) %collective-permute-start.6) | collective-permute-done | bytes 262176 | tf_op jit(solution)/shard_map/ppermute | solution.py:26
  35.2 0.8 collective-permute-start
  36.0 1.1 collective-permute-start.1
  37.2 0.4 collective-permute-start.14
  37.6 2.2 %collective-permute-done.13.p0 = bf16[64,2048]{1,0:T(8,128)(2,1)S(1)} collective-permute-done((bf16[64,2048]{1,0:T(8,128)(2,1)S(1)}, bf16[64,2048]{1,0:T(8,128)(2,1)S(1)}, u32[]{:S(2)}, u32[]{:S(2)}) %collective-permute-start.13) | collective-permute-done | bytes 262176 | tf_op jit(solution)/shard_map/ppermute | solution.py:26
  39.8 0.8 collective-permute-start.15
  40.7 2.9 %collective-permute-done.14.p1 = bf16[64,2048]{1,0:T(8,128)(2,1)S(1)} collective-permute-done((bf16[64,2048]{1,0:T(8,128)(2,1)S(1)}, bf16[64,2048]{1,0:T(8,128)(2,1)S(1)}, u32[]{:S(2)}, u32[]{:S(2)}) %collective-permute-start.14) | collective-permute-done | bytes 262176 | tf_op jit(solution)/shard_map/ppermute | solution.py:26
  43.5 2.1 %collective-permute-start.10 = (bf16[64,2048]{1,0:T(8,128)(2,1)S(1)}, bf16[64,2048]{1,0:T(8,128)(2,1)S(1)}, u32[]{:S(2)}, u32[]{:S(2)}) collective-permute-start(bf16[64,2048]{1,0:T(8,128)(2,1)S(1)} %collective-permute-done.6.p1), channel_id=1, source_target_pairs={{0,34},{1,35},{2,32},{3,33},{4,38},{5,39},{6,36},{7,37},{8,42},{9,... | collective-permute-start | bytes 786440 | tf_op jit(solution)/shard_map/ppermute | solution.py:26
  45.6 1.1 collective-permute-start.16
  46.8 8.9 %shard_map.58 = f32[16,2,8,128]{3,2,1,0:T(8,128)S(1)} custom-call(bf16[64,2048]{1,0:T(8,128)(2,1)S(1)} %collective-permute-done.5.p0, bf16[64,2048]{1,0:T(8,128)(2,1)S(1)} %collective-permute-done.6.p1, bf16[64,2048]{1,0:T(8,128)(2,1)S(1)} %collective-permute-done.7.p2, bf16[64,2048]{1,0:T(8,128)(2,1)S(1)} %collective-permute-done.8.p3, ...), custom_call_target="tpu_custom_call" | custom-call | flops 2147483648 | bytes 8388608 | tf_op jit(solution)/shard_map/pallas_call | solution.py:156
  55.7 0.1 collective-permute-start.11
  55.8 2.2 %collective-permute-start.12 = (bf16[64,2048]{1,0:T(8,128)(2,1)S(1)}, bf16[64,2048]{1,0:T(8,128)(2,1)S(1)}, u32[]{:S(2)}, u32[]{:S(2)}) collective-permute-start(bf16[64,2048]{1,0:T(8,128)(2,1)S(1)} %collective-permute-done.8.p3), channel_id=1, source_target_pairs={{0,34},{1,35},{2,32},{3,33},{4,38},{5,39},{6,36},{7,37},{8,42},{9,... | collective-permute-start | bytes 786440 | tf_op jit(solution)/shard_map/ppermute | solution.py:26
  58.0 1.3 %collective-permute-start.9 = (bf16[64,2048]{1,0:T(8,128)(2,1)S(1)}, bf16[64,2048]{1,0:T(8,128)(2,1)S(1)}, u32[]{:S(2)}, u32[]{:S(2)}) collective-permute-start(bf16[64,2048]{1,0:T(8,128)(2,1)S(1)} %collective-permute-done.5.p0), channel_id=1, source_target_pairs={{0,32},{1,33},{2,34},{3,35},{4,36},{5,37},{6,38},{7,39},{8,40},{9,... | collective-permute-start | bytes 786440 | tf_op jit(solution)/shard_map/ppermute | solution.py:26
  59.3 8.9 %shard_map.57 = f32[16,2,8,128]{3,2,1,0:T(8,128)S(1)} custom-call(bf16[64,2048]{1,0:T(8,128)(2,1)S(1)} %get-tuple-element.7.p0, bf16[64,2048]{1,0:T(8,128)(2,1)S(1)} %get-tuple-element.8.p1, bf16[64,2048]{1,0:T(8,128)(2,1)S(1)} %collective-permute-done.p2, bf16[64,2048]{1,0:T(8,128)(2,1)S(1)} %collective-permute-done.1.p3, ...), custom_call_target="tpu_custom_call" | custom-call | flops 2147483648 | bytes 8388608 | tf_op jit(solution)/shard_map/pallas_call | solution.py:156
  68.2 8.9 %shard_map.60 = f32[16,2,8,128]{3,2,1,0:T(8,128)S(1)} custom-call(bf16[64,2048]{1,0:T(8,128)(2,1)S(1)} %collective-permute-done.13.p0, bf16[64,2048]{1,0:T(8,128)(2,1)S(1)} %collective-permute-done.14.p1, bf16[64,2048]{1,0:T(8,128)(2,1)S(1)} %collective-permute-done.15.p2, bf16[64,2048]{1,0:T(8,128)(2,1)S(1)} %collective-permute-done.16.p3, ...), custom_call_target="tpu_custom_call" | custom-call | flops 2147483648 | bytes 8388608 | tf_op jit(solution)/shard_map/pallas_call | solution.py:156
  77.1 8.9 %shard_map.59 = f32[16,2,8,128]{3,2,1,0:T(8,128)S(1)} custom-call(bf16[64,2048]{1,0:T(8,128)(2,1)S(1)} %collective-permute-done.9.p0, bf16[64,2048]{1,0:T(8,128)(2,1)S(1)} %collective-permute-done.10.p1, bf16[64,2048]{1,0:T(8,128)(2,1)S(1)} %collective-permute-done.11.p2, bf16[64,2048]{1,0:T(8,128)(2,1)S(1)} %collective-permute-done.12.p3, ...), custom_call_target="tpu_custom_call" | custom-call | flops 2147483648 | bytes 8388608 | tf_op jit(solution)/shard_map/pallas_call | solution.py:156
  86.0 0.8 pad_maximum_fusion
  86.8 10.7 %all-to-all-start = ((f32[32,32,128]{2,1,0:T(8,128)}), f32[32,32,128]{2,1,0:T(8,128)S(1)}, u32[]{:S(2)}, u32[]{:S(2)}) async-start(f32[32,32,128]{2,1,0:T(8,128)} %bitcast.7), calls=%async_computation | async-start | bytes 1048576 | tf_op jit(solution)/shard_map/all_to_all | solution.py:289
  97.5 0.1 and_convert_fusion.2
  97.6 0.1 reshape.260
  97.7 0.1 copy.9.pick_ref
  98.0 0.1 select_reduce_fusion.3
  98.1 0.1 copy.10.atoms_ref
  98.2 17.0 %all-to-all-done = f32[32,32,128]{2,1,0:T(8,128)S(1)} async-done(((f32[32,32,128]{2,1,0:T(8,128)}), f32[32,32,128]{2,1,0:T(8,128)S(1)}, u32[]{:S(2)}, u32[]{:S(2)}) %all-to-all-start) | async-done | bytes 524320 | tf_op jit(solution)/shard_map/all_to_all | solution.py:289
  115.2 1.6 %shard_map.61 = f32[32,2048]{1,0:T(8,128)} custom-call(s32[16]{0:T(128)S(1)} %add.247.column_ref, f32[16,2,32,128]{3,2,1,0:T(8,128)S(1)} %bitcast.23, bf16[64,128]{1,0:T(8,128)(2,1)S(1)} %copy.9.pick_ref, f32[32,1]{1,0:T(8,128)S(1)} %copy.10.atoms_ref), custom_call_target="tpu_custom_call" | custom-call | tf_op jit(solution)/shard_map/pallas_call | solution.py:199
  (49 shorter events, 0.8 us)
Async XLA Ops:
  0.8 23.9 %collective-permute-start.3 = (bf16[16,2048]{1,0:T(8,128)(2,1)S(1)}, bf16[16,2048]{1,0:T(8,128)(2,1)S(1)}, u32[]{:S(2)}, u32[]{:S(2)}) collective-permute-start(bf16[16,2048]{1,0:T(8,128)(2,1)S(1)} %slice.18), channel_id=1, source_target_pairs={{1,2},{3,4},{5,6},{7,8},{9,10},{11,12},{13,14},{15,16},{17,18},{19... | collective-permute-start | bytes 196616 | tf_op jit(solution)/shard_map/ppermute | solution.py:26
  2.1 22.9 %collective-permute-start.4 = (bf16[16,2048]{1,0:T(8,128)(2,1)S(1)}, bf16[16,2048]{1,0:T(8,128)(2,1)S(1)}, u32[]{:S(2)}, u32[]{:S(2)}) collective-permute-start(bf16[16,2048]{1,0:T(8,128)(2,1)S(1)} %slice.18), channel_id=1, source_target_pairs={{1,3},{3,5},{5,7},{7,9},{9,11},{11,13},{13,15},{15,17},{17,19},{19... | collective-permute-start | bytes 196616 | tf_op jit(solution)/shard_map/ppermute | solution.py:26
  2.8 1.2 %copy-start.1 = (bf16[256,2048]{1,0:T(8,128)(2,1)S(1)}, bf16[256,2048]{1,0:T(8,128)(2,1)}, u32[]{:S(2)}) copy-start(bf16[256,2048]{1,0:T(8,128)(2,1)} %desc_ref.2) | copy-start | bytes 3145732
  4.3 23.8 %collective-permute-start.5 = (bf16[64,2048]{1,0:T(8,128)(2,1)S(1)}, bf16[64,2048]{1,0:T(8,128)(2,1)S(1)}, u32[]{:S(2)}, u32[]{:S(2)}) collective-permute-start(bf16[64,2048]{1,0:T(8,128)(2,1)S(1)} %get-tuple-element.7.p0), channel_id=1, source_target_pairs={{0,64},{1,65},{2,66},{3,67},{4,68},{5,69},{6,70},{7,71},{8,72},{9,... | collective-permute-start | bytes 786440 | tf_op jit(solution)/shard_map/ppermute | solution.py:26
  5.9 30.1 %collective-permute-start.7 = (bf16[64,2048]{1,0:T(8,128)(2,1)S(1)}, bf16[64,2048]{1,0:T(8,128)(2,1)S(1)}, u32[]{:S(2)}, u32[]{:S(2)}) collective-permute-start(bf16[64,2048]{1,0:T(8,128)(2,1)S(1)} %get-tuple-element.7.p0), channel_id=1, source_target_pairs={{0,192},{1,193},{2,194},{3,195},{4,196},{5,197},{6,198},{7,199},{8... | collective-permute-start | bytes 786440 | tf_op jit(solution)/shard_map/ppermute | solution.py:26
  7.6 2.2 %copy-start = (bf16[1024,2048]{1,0:T(8,128)(2,1)S(1)}, bf16[1024,2048]{1,0:T(8,128)(2,1)}, u32[]{:S(2)}) copy-start(bf16[1024,2048]{1,0:T(8,128)(2,1)} %desc_ref.3) | copy-start | bytes 12582916
  9.8 10.5 %copy-start.2 = (s32[1,1024]{1,0:T(1,128)S(1)}, s32[1,1024]{1,0:T(1,128)}, u32[]{:S(2)}) copy-start(s32[1,1024]{1,0:T(1,128)} %param.7) | copy-start | bytes 12292
  9.8 14.1 %copy-start.3 = (s32[1,1024]{1,0:T(1,128)S(1)}, s32[1,1024]{1,0:T(1,128)}, u32[]{:S(2)}) copy-start(s32[1,1024]{1,0:T(1,128)} %param.8) | copy-start | bytes 12292
  14.1 31.6 %collective-permute-start.2 = (bf16[1024,2048]{1,0:T(8,128)(2,1)}, bf16[1024,2048]{1,0:T(8,128)(2,1)}, u32[]{:S(2)}, u32[]{:S(2)}) collective-permute-start(bf16[1024,2048]{1,0:T(8,128)(2,1)} %shard_map.56.own), channel_id=1, source_target_pairs={{0,1},{1,0},{2,3},{3,2},{4,5},{5,4},{6,7},{7,6},{8,9},{9,8},{10,11... | collective-permute-start | bytes 12582920 | tf_op jit(solution)/shard_map/ppermute | solution.py:26
  24.7 10.5 %collective-permute-start.6 = (bf16[64,2048]{1,0:T(8,128)(2,1)S(1)}, bf16[64,2048]{1,0:T(8,128)(2,1)S(1)}, u32[]{:S(2)}, u32[]{:S(2)}) collective-permute-start(bf16[64,2048]{1,0:T(8,128)(2,1)S(1)} %get-tuple-element.8.p1), channel_id=1, source_target_pairs={{0,64},{1,65},{2,66},{3,67},{4,68},{5,69},{6,70},{7,71},{8,72},{9,... | collective-permute-start | bytes 786440 | tf_op jit(solution)/shard_map/ppermute | solution.py:26
  25.0 12.1 %collective-permute-start.8 = (bf16[64,2048]{1,0:T(8,128)(2,1)S(1)}, bf16[64,2048]{1,0:T(8,128)(2,1)S(1)}, u32[]{:S(2)}, u32[]{:S(2)}) collective-permute-start(bf16[64,2048]{1,0:T(8,128)(2,1)S(1)} %get-tuple-element.8.p1), channel_id=1, source_target_pairs={{0,192},{1,193},{2,194},{3,195},{4,196},{5,197},{6,198},{7,199},{8... | collective-permute-start | bytes 786440 | tf_op jit(solution)/shard_map/ppermute | solution.py:26
  28.0 11.8 %collective-permute-start.13 = (bf16[64,2048]{1,0:T(8,128)(2,1)S(1)}, bf16[64,2048]{1,0:T(8,128)(2,1)S(1)}, u32[]{:S(2)}, u32[]{:S(2)}) collective-permute-start(bf16[64,2048]{1,0:T(8,128)(2,1)S(1)} %collective-permute-done.5.p0), channel_id=1, source_target_pairs={{0,64},{1,65},{2,66},{3,67},{4,68},{5,69},{6,70},{7,71},{8,72},{9,... | collective-permute-start | bytes 786440 | tf_op jit(solution)/shard_map/ppermute | solution.py:26
  35.2 20.5 %collective-permute-start = (bf16[64,2048]{1,0:T(8,128)(2,1)S(1)}, bf16[64,2048]{1,0:T(8,128)(2,1)S(1)}, u32[]{:S(2)}, u32[]{:S(2)}) collective-permute-start(bf16[64,2048]{1,0:T(8,128)(2,1)S(1)} %get-tuple-element.7.p0), channel_id=1, source_target_pairs={{0,32},{1,33},{2,34},{3,35},{4,36},{5,37},{6,38},{7,39},{8,40},{9,... | collective-permute-start | bytes 786440 | tf_op jit(solution)/shard_map/ppermute | solution.py:26
  36.0 19.7 %collective-permute-start.1 = (bf16[64,2048]{1,0:T(8,128)(2,1)S(1)}, bf16[64,2048]{1,0:T(8,128)(2,1)S(1)}, u32[]{:S(2)}, u32[]{:S(2)}) collective-permute-start(bf16[64,2048]{1,0:T(8,128)(2,1)S(1)} %get-tuple-element.8.p1), channel_id=1, source_target_pairs={{0,34},{1,35},{2,32},{3,33},{4,38},{5,39},{6,36},{7,37},{8,42},{9,... | collective-permute-start | bytes 786440 | tf_op jit(solution)/shard_map/ppermute | solution.py:26
  37.2 6.4 %collective-permute-start.14 = (bf16[64,2048]{1,0:T(8,128)(2,1)S(1)}, bf16[64,2048]{1,0:T(8,128)(2,1)S(1)}, u32[]{:S(2)}, u32[]{:S(2)}) collective-permute-start(bf16[64,2048]{1,0:T(8,128)(2,1)S(1)} %collective-permute-done.8.p3), channel_id=1, source_target_pairs={{0,192},{1,193},{2,194},{3,195},{4,196},{5,197},{6,198},{7,199},{8... | collective-permute-start | bytes 786440 | tf_op jit(solution)/shard_map/ppermute | solution.py:26
  39.8 18.1 %collective-permute-start.15 = (bf16[64,2048]{1,0:T(8,128)(2,1)S(1)}, bf16[64,2048]{1,0:T(8,128)(2,1)S(1)}, u32[]{:S(2)}, u32[]{:S(2)}) collective-permute-start(bf16[64,2048]{1,0:T(8,128)(2,1)S(1)} %collective-permute-done.13.p0), channel_id=1, source_target_pairs={{0,32},{1,33},{2,34},{3,35},{4,36},{5,37},{6,38},{7,39},{8,40},{9,... | collective-permute-start | bytes 786440 | tf_op jit(solution)/shard_map/ppermute | solution.py:26
  43.5 33.5 %collective-permute-start.10 = (bf16[64,2048]{1,0:T(8,128)(2,1)S(1)}, bf16[64,2048]{1,0:T(8,128)(2,1)S(1)}, u32[]{:S(2)}, u32[]{:S(2)}) collective-permute-start(bf16[64,2048]{1,0:T(8,128)(2,1)S(1)} %collective-permute-done.6.p1), channel_id=1, source_target_pairs={{0,34},{1,35},{2,32},{3,33},{4,38},{5,39},{6,36},{7,37},{8,42},{9,... | collective-permute-start | bytes 786440 | tf_op jit(solution)/shard_map/ppermute | solution.py:26
  45.6 22.5 %collective-permute-start.16 = (bf16[64,2048]{1,0:T(8,128)(2,1)S(1)}, bf16[64,2048]{1,0:T(8,128)(2,1)S(1)}, u32[]{:S(2)}, u32[]{:S(2)}) collective-permute-start(bf16[64,2048]{1,0:T(8,128)(2,1)S(1)} %collective-permute-done.14.p1), channel_id=1, source_target_pairs={{0,34},{1,35},{2,32},{3,33},{4,38},{5,39},{6,36},{7,37},{8,42},{9,... | collective-permute-start | bytes 786440 | tf_op jit(solution)/shard_map/ppermute | solution.py:26
  55.7 21.4 %collective-permute-start.11 = (bf16[64,2048]{1,0:T(8,128)(2,1)S(1)}, bf16[64,2048]{1,0:T(8,128)(2,1)S(1)}, u32[]{:S(2)}, u32[]{:S(2)}) collective-permute-start(bf16[64,2048]{1,0:T(8,128)(2,1)S(1)} %collective-permute-done.7.p2), channel_id=1, source_target_pairs={{0,32},{1,33},{2,34},{3,35},{4,36},{5,37},{6,38},{7,39},{8,40},{9,... | collective-permute-start | bytes 786440 | tf_op jit(solution)/shard_map/ppermute | solution.py:26
  55.8 21.3 %collective-permute-start.12 = (bf16[64,2048]{1,0:T(8,128)(2,1)S(1)}, bf16[64,2048]{1,0:T(8,128)(2,1)S(1)}, u32[]{:S(2)}, u32[]{:S(2)}) collective-permute-start(bf16[64,2048]{1,0:T(8,128)(2,1)S(1)} %collective-permute-done.8.p3), channel_id=1, source_target_pairs={{0,34},{1,35},{2,32},{3,33},{4,38},{5,39},{6,36},{7,37},{8,42},{9,... | collective-permute-start | bytes 786440 | tf_op jit(solution)/shard_map/ppermute | solution.py:26
  58.0 19.1 %collective-permute-start.9 = (bf16[64,2048]{1,0:T(8,128)(2,1)S(1)}, bf16[64,2048]{1,0:T(8,128)(2,1)S(1)}, u32[]{:S(2)}, u32[]{:S(2)}) collective-permute-start(bf16[64,2048]{1,0:T(8,128)(2,1)S(1)} %collective-permute-done.5.p0), channel_id=1, source_target_pairs={{0,32},{1,33},{2,34},{3,35},{4,36},{5,37},{6,38},{7,39},{8,40},{9,... | collective-permute-start | bytes 786440 | tf_op jit(solution)/shard_map/ppermute | solution.py:26
  77.0 20.8 %copy-start.4 = (s32[8,1]{0,1:T(1,128)S(1)}, s32[8,1]{0,1:T(1,128)}, u32[]{:S(2)}) copy-start(s32[8,1]{0,1:T(1,128)} %constant.127) | copy-start | bytes 100
  77.0 20.8 %copy-start.5 = (s32[8,1]{0,1:T(1,128)S(1)}, s32[8,1]{0,1:T(1,128)}, u32[]{:S(2)}) copy-start(s32[8,1]{0,1:T(1,128)} %constant.128) | copy-start | bytes 100
  86.8 28.4 %all-to-all-start = ((f32[32,32,128]{2,1,0:T(8,128)}), f32[32,32,128]{2,1,0:T(8,128)S(1)}, u32[]{:S(2)}, u32[]{:S(2)}) async-start(f32[32,32,128]{2,1,0:T(8,128)} %bitcast.7), calls=%async_computation | async-start | bytes 1048576 | tf_op jit(solution)/shard_map/all_to_all | solution.py:289

commit v2 on v0

v2 whole, which is shorter than its diff:
```python
import functools

import jax
import jax.numpy as jnp
from jax import lax
from jax.experimental import pallas as pl
from jax.experimental.pallas import tpu as pltpu
from jax.sharding import PartitionSpec as P

Y, XL, Z, XH, CORE = 4, 2, 8, 2, 2
CHIPS = Z * XH
ROWS = CHIPS * CORE
KEEP = 4
HELD = ROWS * KEEP
HELD_ROWS = HELD + 8
SENT = 8 * KEEP + 8
LANES = 128
MIB = 1 << 20
SHIFTS = ((0, 0), (0, 1), (3, 0), (1, 0), (3, 1), (1, 1), (2, 0), (2, 1))
STEPS, LEAST, ZERO = 512.0, 126.0, 32768

VMEM = pl.BlockSpec(memory_space=pltpu.VMEM)
ANY = pl.BlockSpec(memory_space=pl.ANY)


def place(y, xl, z, xh, core):
    return (((y % Y * XL + xl) * Z + z % Z) * XH + xh) * CORE + core


def move(array, to):
    pairs = []
    for y in range(Y):
        for xl in range(XL):
            for z in range(Z):
                for xh in range(XH):
                    for core in range(CORE):
                        target = to(y, xl, z, xh, core)
                        if target is not None:
                            pairs.append((place(y, xl, z, xh, core), place(*target)))
    return lax.ppermute(array, ("sparse", "rows"), pairs)


def up(y, xl, z, xh, core):
    return y + 1, xl, z, xh, core


def down(y, xl, z, xh, core):
    return y - 1, xl, z, xh, core


def across(y, xl, z, xh, core):
    return y, 1 - xl, z, (xh + core) % XH, core


def onward(y, xl, z, xh, core):
    return (y + 1 if core == 0 else y - 1), xl, z, xh, core


def other_core(y, xl, z, xh, core):
    return y, xl, z, xh, 1 - core


def unit(desc):
    values = desc.astype(jnp.float32)
    scale = 1.0 / jnp.sqrt(jnp.sum(values * values, axis=1, keepdims=True) + 1e-06)
    return (values * scale).astype(jnp.bfloat16)


def in_hbm(array):
    return pltpu.with_memory_space_constraint(array, pltpu.HBM)


def in_vmem(array):
    return pltpu.with_memory_space_constraint(array, pltpu.VMEM)


def params(mib):
    return pltpu.CompilerParams(vmem_limit_bytes=mib * MIB)


def cost(flops, moved):
    return pl.CostEstimate(flops=flops, bytes_accessed=moved, transcendentals=0)


def sparse_kernel(desc_ref, half_ref, raw, sem):
    half = half_ref.shape[0]
    at = pl.multiple_of(lax.axis_index("rows") % CORE * half, half)
    copy = pltpu.make_async_copy(desc_ref.at[pl.ds(at, half)], raw, sem)
    copy.start()
    copy.wait()
    half_ref[...] = unit(raw[...])


def sparse_unit(desc):
    rows, width = desc.shape
    half = rows // CORE
    return pl.pallas_call(
        sparse_kernel,
        in_specs=[ANY],
        out_specs=VMEM,
        out_shape=jax.ShapeDtypeStruct((half, width), jnp.bfloat16),
        scratch_shapes=[pltpu.VMEM((half, width), jnp.bfloat16), pltpu.SemaphoreType.DMA],
        compiler_params=params(8),
        cost_estimate=cost(4 * half * width, 4 * half * width),
        name="sparse_unit",
    )(in_hbm(desc))


def env_kernel(own_desc, other_desc, *refs):
    own_ref, other_ref, raw, sems = refs[-4:]
    rows = own_desc.shape[0]
    tiles = sems.shape[0] // 2
    tile = rows // tiles
    steps = []
    for env, (desc, out) in enumerate(((own_desc, own_ref), (other_desc, other_ref))):
        for i in range(tiles):
            copy = pltpu.make_async_copy(
                desc.at[pl.ds(i * tile, tile)],
                raw.at[env, pl.ds(i * tile, tile)],
                sems.at[env * tiles + i],
            )
            steps.append((copy, env, out, slice(i * tile, (i + 1) * tile)))
    for copy, *_ in steps:
        copy.start()
    for copy, env, out, to in steps:
        copy.wait()
        out[to] = unit(raw[env, to])


def env_unit(own, other, after):
    rows, width = own.shape
    whole = jax.ShapeDtypeStruct((rows, width), jnp.bfloat16)
    return pl.pallas_call(
        env_kernel,
        in_specs=[ANY] * (2 + len(after)),
        out_specs=[VMEM] * 2,
        out_shape=[whole, whole],
        scratch_shapes=[
            pltpu.VMEM((CORE, rows, width), jnp.bfloat16),
            pltpu.SemaphoreType.DMA((8,)),
        ],
        compiler_params=params(24),
        cost_estimate=cost(16 * rows * width, 8 * rows * width),
        name="env_unit",
    )(in_hbm(own), other, *after)


def choose_kernel(up_ref, down_ref, *refs):
    first = lax.axis_index("rows") % CORE == 0
    refs[-1][...] = jnp.where(first, up_ref[...], down_ref[...])


def choose(from_up, from_down, after):
    return pl.pallas_call(
        choose_kernel,
        in_specs=[VMEM, VMEM] + [ANY] * len(after),
        out_specs=VMEM,
        out_shape=jax.ShapeDtypeStruct(from_up.shape, from_up.dtype),
        compiler_params=params(4),
        cost_estimate=cost(0, 6 * from_up.size),
        name="choose",
    )(from_up, from_down, *after)


def hold_kernel(array_ref, *refs):
    refs[-1][...] = array_ref[...]


def hold(array, after):
    return pl.pallas_call(
        hold_kernel,
        in_specs=[VMEM] + [ANY] * len(after),
        out_specs=VMEM,
        out_shape=jax.ShapeDtypeStruct(array.shape, array.dtype),
        compiler_params=params(4),
        cost_estimate=cost(0, 4 * array.size),
        name="hold",
    )(array, *after)


def book_kernel(
    extra_ref,
    slots_ref,
    own_ref,
    other_ref,
    inverse_ref,
    more_owner_ref,
    pick_ref,
    pick_more_ref,
    *,
    env_rows,
):
    groups = extra_ref.shape[1]
    parts = groups // LANES
    atom_min = env_rows // (2 * (groups // ROWS))
    chip_rows = CORE * env_rows
    my_row = lax.axis_index("rows")
    core = my_row % CORE
    chip = my_row // CORE
    base = chip * chip_rows

    def rows_of(ref):
        return jnp.concatenate([ref[:, i * LANES : (i + 1) * LANES] for i in range(parts)], axis=0)

    atoms = rows_of(extra_ref) + (atom_min - 1)
    slots = rows_of(slots_ref)
    lane_i = lax.broadcasted_iota(jnp.int32, (LANES, LANES), 0)
    lane_j = lax.broadcasted_iota(jnp.int32, (LANES, LANES), 1)
    upto = (lane_i <= lane_j).astype(jnp.float32)
    along = jnp.dot(
        atoms.astype(jnp.float32).astype(jnp.bfloat16),
        upto.astype(jnp.bfloat16),
        preferred_element_type=jnp.float32,
    )
    rows_total = along[:, LANES - 1 :].astype(jnp.int32)
    ends = along.astype(jnp.int32)
    part = lax.broadcasted_iota(jnp.int32, (parts, LANES), 0)
    for i in range(parts - 1):
        ends = ends + jnp.where(part > i, rows_total[i : i + 1, :], 0)
    starts = ends - atoms

    found = (ends <= base).astype(jnp.int32)
    first = jnp.sum(jnp.sum(found, axis=0, keepdims=True), axis=1, keepdims=True)

    row = lax.broadcasted_iota(jnp.int32, (HELD_ROWS, 1), 0)
    held = first + ((row // KEEP - first) & (ROWS - 1)) + ROWS * (row % KEEP)
    held = jnp.where(row < HELD, held, jnp.where(row == HELD, first + HELD, -1))
    more_owner_ref[...] = jnp.broadcast_to((first + HELD) & (ROWS - 1), more_owner_ref.shape)
    lane = lax.broadcasted_iota(jnp.int32, (HELD_ROWS, LANES), 1)
    found_start = jnp.zeros((HELD_ROWS, LANES), jnp.int32)
    found_end = jnp.zeros((HELD_ROWS, LANES), jnp.int32)
    for i in range(parts):
        here = held == lane + i * LANES
        found_start = jnp.where(here, starts[i : i + 1, :], found_start)
        found_end = jnp.where(here, ends[i : i + 1, :], found_end)
    start = jnp.sum(found_start, axis=1, keepdims=True)
    end = jnp.sum(found_end, axis=1, keepdims=True)
    inverse_ref[...] = 1.0 / jnp.maximum(end - start, 1).astype(jnp.float32)
    lower = jnp.maximum(start, base)

    def member(begin, count):
        position = begin + lax.broadcasted_iota(jnp.int32, (HELD_ROWS, count), 1)
        inside = (position >= lower) & (position < end)
        return inside.astype(jnp.float32).astype(jnp.bfloat16)

    own_ref[...] = member(base + core * env_rows, env_rows)
    other_ref[...] = member(base + (1 - core) * env_rows, env_rows)

    ends_down = ends.astype(jnp.float32).T.astype(jnp.int32)
    slots_down = slots.astype(jnp.float32).T.astype(jnp.int32)
    from_lane = lax.broadcasted_iota(jnp.int32, (1, LANES), 1)
    limit = (from_lane // (2 * KEEP)) * chip_rows
    ended = jnp.zeros((LANES, LANES), jnp.int32)
    for i in range(parts):
        ended = ended + (ends_down[:, i : i + 1] <= limit).astype(jnp.int32)
    firsts = jnp.sum(ended, axis=0, keepdims=True)
    sent = firsts + ((my_row - firsts) & (ROWS - 1)) + ROWS * (from_lane % KEEP)
    below = lax.broadcasted_iota(jnp.int32, (LANES, LANES), 0)
    more = firsts + HELD

    def slot_of(structure):
        found = jnp.zeros((LANES, LANES), jnp.int32)
        for i in range(parts):
            found = jnp.where(structure == below + i * LANES, slots_down[:, i : i + 1] + 1, found)
        return jnp.sum(found, axis=0, keepdims=True) - 1

    def picks(ref, slot, part):
        count = groups // ROWS
        target = lax.broadcasted_iota(jnp.int32, ref.shape, 0)
        chosen = (target % count == slot) & (target // count == part)
        ref[...] = chosen.astype(jnp.float32).astype(jnp.bfloat16)

    picks(pick_ref, slot_of(sent), (from_lane // KEEP) % 2)
    more_slot = jnp.where((more & (ROWS - 1)) == my_row, slot_of(more), -1)
    picks(pick_more_ref, more_slot, from_lane % 8)


def book(extra_atoms, owner_slots, env_rows):
    str_dev = extra_atoms.shape[1] // ROWS

    return pl.pallas_call(
        functools.partial(book_kernel, env_rows=env_rows),
        in_specs=[VMEM, VMEM],
        out_specs=[VMEM] * 6,
        out_shape=[
            jax.ShapeDtypeStruct((HELD_ROWS, env_rows), jnp.bfloat16),
            jax.ShapeDtypeStruct((HELD_ROWS, env_rows), jnp.bfloat16),
            jax.ShapeDtypeStruct((HELD_ROWS, 1), jnp.float32),
            jax.ShapeDtypeStruct((1, LANES), jnp.int32),
            jax.ShapeDtypeStruct((2 * str_dev, LANES), jnp.bfloat16),
            jax.ShapeDtypeStruct((8 * str_dev, LANES), jnp.bfloat16),
        ],
        compiler_params=params(8),
        cost_estimate=cost(1 << 22, 1 << 20),
        name="book",
    )(extra_atoms, owner_slots)


def power_parts(env, block):
    inner = lax.dot_general(env, block, (((1,), (1,)), ((), ())), preferred_element_type=jnp.float32)
    square = inner * inner
    kernel = square * square
    high = kernel.astype(jnp.bfloat16)
    return high, (kernel - high.astype(jnp.float32)).astype(jnp.bfloat16)


def block_sums(a, b, own, other, of_own, of_other, block, high, low):
    half = a.shape[0]
    block[:half] = a[...]
    block[half:] = b[...]
    rows = own.shape[0]
    tile = 512
    for begin, env in ((0, own), (rows, other)):
        for i in range(0, rows, tile):
            to = slice(begin + i, begin + i + tile)
            high[to], low[to] = power_parts(env[i : i + tile], block[...])

    def dot(member, part):
        return jnp.dot(member[...], part, preferred_element_type=jnp.float32)

    return (
        dot(of_own, high[:rows])
        + dot(of_own, low[:rows])
        + dot(of_other, high[rows:])
        + dot(of_other, low[rows:])
    )


def early_call(a, b, own, other, of_own, of_other, out, block, high, low):
    out[...] = block_sums(a, b, own, other, of_own, of_other, block, high, low)


def encode(sums):
    position = (jnp.log2(jnp.maximum(sums, 1e-37)) + LEAST) * STEPS
    code = jnp.clip(jnp.round(position), 0.0, 65534.0).astype(jnp.int32) + (1 - ZERO)
    return jnp.where(sums >= 2.0**-126, code, -ZERO)


def decode(codes):
    code = codes.astype(jnp.int32) + (ZERO - 1)
    return jnp.where(code < 0, 0.0, jnp.exp2(code.astype(jnp.float32) * (1.0 / STEPS) - LEAST))


def last_call(sums_0, sums_1, sums_2, inverse, more_owner, *refs):
    *operands, out_ref, block, high, low = refs
    last = block_sums(*operands, block, high, low)
    means = [part * inverse[...] for part in (sums_0[...], sums_1[...], sums_2[...], last)]
    tiles = (ROWS // 2, 2 * KEEP, LANES)
    lower = lax.broadcasted_iota(jnp.int32, tiles, 1) < KEEP
    owner = 2 * lax.broadcasted_iota(jnp.int32, tiles, 0)
    packed = ([], [])
    more = []
    for mean in means:
        both = encode(mean[:HELD]).reshape(ROWS // 2, 2 * KEEP, 2 * LANES)
        left, right = both[:, :, :LANES], both[:, :, LANES:]
        packed[0].append(jnp.where(lower, left, jnp.roll(right, KEEP, axis=1)))
        packed[1].append(jnp.where(lower, jnp.roll(left, KEEP, axis=1), right))
        more += [mean[HELD : HELD + 1, :LANES], mean[HELD : HELD + 1, LANES:]]
    codes = encode(jnp.concatenate(more, axis=0)).reshape(1, 8, LANES)
    for i in range(2):
        here = owner + i == more_owner[...].reshape(1, 1, LANES)
        packed[i].append(jnp.where(here, codes, -ZERO))
    rows = packed[0] + packed[1]
    for i in range(0, len(rows), 2):
        both = jnp.concatenate(rows[i : i + 2], axis=1)
        out_ref[:, 8 * i : 8 * i + 16] = both.astype(jnp.int16)


def call(kernel, first, pieces, envs, members, out_shape):
    own, other = envs
    rows, width = own.shape
    columns = 2 * LANES
    operands = (*first, *pieces, in_vmem(own), in_vmem(other), *members)
    return pl.pallas_call(
        kernel,
        in_specs=[VMEM] * len(operands),
        out_specs=VMEM,
        out_shape=out_shape,
        scratch_shapes=[
            pltpu.VMEM((columns, width), jnp.bfloat16),
            pltpu.VMEM((2 * rows, columns), jnp.bfloat16),
            pltpu.VMEM((2 * rows, columns), jnp.bfloat16),
        ],
        compiler_params=params(16),
        cost_estimate=cost(4 * rows * width * columns, 4 * rows * width),
        name=kernel.__name__,
    )(*operands)


def combine_kernel(got_ref, pick_ref, pick_more_ref, out_ref):
    block = lax.axis_index("sparse")
    y, xl = block // XL, block % XL
    count = out_ref.shape[0]
    tiles = []
    for i in range(CORE * SENT // 16):
        values = decode(got_ref[:, 16 * i : 16 * (i + 1), :])
        for j in range(2):
            tiles.append(values[:, 8 * j : 8 * (j + 1), :].reshape(8 * CHIPS, LANES))

    def picked(pick, tile):
        high = tile.astype(jnp.bfloat16)
        low = (tile - high.astype(jnp.float32)).astype(jnp.bfloat16)
        return jnp.dot(pick, high, preferred_element_type=jnp.float32) + jnp.dot(
            pick, low, preferred_element_type=jnp.float32
        )

    for core in range(CORE):
        *held, more = tiles[core * SENT // 8 : (core + 1) * SENT // 8]
        more = picked(pick_more_ref[...], more)
        for i, tile in enumerate(held):
            sums = picked(pick_ref[...], tile) + more[2 * i * count : 2 * (i + 1) * count]
            for half in range(2):
                dy, dx = SHIFTS[2 * i + half]
                column = ((y + dy) % Y * XL + (xl + dx) % XL) * CORE + core
                at = pl.multiple_of(column * LANES, LANES)
                out_ref[:, pl.ds(at, LANES)] = sums[half * count : (half + 1) * count]


def combine(got, pick, pick_more, width):
    return pl.pallas_call(
        combine_kernel,
        in_specs=[VMEM, VMEM, VMEM],
        out_specs=VMEM,
        out_shape=jax.ShapeDtypeStruct((pick.shape[0] // 2, width), jnp.float32),
        compiler_params=params(8),
        name="combine",
    )(got, pick, pick_more)


def on_device(env_desc, sparse_desc, extra_atoms, owner_slots):
    env_rows, _ = env_desc.shape
    width = sparse_desc.shape[0] * Y * XL
    other_desc = move(env_desc, other_core)
    half = sparse_unit(sparse_desc)
    from_up, from_down = move(half, up), move(half, down)
    near = move(half, across)
    *members, inverse, more_owner, pick, pick_more = book(extra_atoms, owner_slots, env_rows)
    envs = env_unit(env_desc, other_desc, (near, inverse))
    sums = jax.ShapeDtypeStruct((HELD_ROWS, 2 * LANES), jnp.float32)
    sums_0 = call(early_call, (), (half, near), envs, members, sums)
    far = move(choose(from_up, from_down, (sums_0,)), onward)
    near_up, near_down = move(from_up, across), move(from_down, across)
    sums_1 = call(early_call, (), (from_up, from_down), envs, members, sums)
    near_far = move(hold(far, (sums_1,)), across)
    sums_2 = call(early_call, (), (near_up, near_down), envs, members, sums)
    codes = call(
        last_call,
        (sums_0, sums_1, sums_2, inverse, more_owner),
        (far, near_far),
        envs,
        members,
        jax.ShapeDtypeStruct((ROWS // 2, 2 * SENT, LANES), jnp.int16),
    )
    got = lax.all_to_all(codes.reshape(ROWS, SENT, LANES), "rows", 0, 0, tiled=True)
    return combine(got.reshape(CHIPS, CORE * SENT, LANES), pick, pick_more, width)


def solution(mesh):
    placed = (P(("sparse", "rows"), None), P("sparse", None), P("sparse", None), P("sparse", None))
    return jax.shard_map(
        on_device,
        mesh=mesh,
        in_specs=placed,
        out_specs=P(("sparse", "rows"), None),
        check_vma=False,
    )
```

time: 354 us -> 71.1 us (0.20)
  waiting for transfers between devices: 292 us -> 14.3 us
  blocking collectives: 0 us -> 26.6 us
  matrix products: 20.4 us -> 0 us
  Pallas kernels: 0 us -> 19.9 us
  other arithmetic: 16.7 us -> 0 us
  between operations: 13.5 us -> 0.09 us
    reduce_scatter x1 -> x0, waiting for transfers between devices: 156 us -> none  [on_device(): lax.psum_scatter(jnp.dot(pick, partial_sums, precision=lax.Precision.HIGH...]
    ppermute x7 -> x8, waiting for transfers between devices: 136 us -> 14.3 us  [move(): return lax.ppermute(array, ('sparse', 'rows'), pairs)]
    all_to_all x0 -> x1, blocking collectives: none -> 26.6 us  [on_device(): lax.all_to_all(codes.reshape(ROWS, SENT, LANES), 'rows', 0, 0, tiled=True)]
    dot_general x10 -> x0, matrix products: 20.4 us -> none  [the longest x8 12.9 us: power_kernel(): lax.dot_general(env_unit, block, (((1,), (1,)), ((), ())), preferred_elem...]
    pallas_call x0 -> x10, Pallas kernels: none -> 19.9 us  [the longest x4 12.1 us: call(): pl.pallas_call(kernel, in_specs=[VMEM] * len(operands), out_specs=VMEM, o...]
    reduce_sum x5 -> x0, other arithmetic: 6.41 us -> none  [the longest x2 4.58 us: unit_rows(): jnp.sum(values * values, axis=1, keepdims=True) + 1e-06]
    convert_element_type x3 -> x0, other arithmetic: 5.55 us -> none  [the longest x2 5.54 us: unit_rows(): (values / jnp.sqrt(jnp.sum(values * values, axis=1, keepdims=True) + 1e-0...]
    ppermute x7 -> x8, starting transfers between devices: 8.37 us -> 8.62 us  [move(): return lax.ppermute(array, ('sparse', 'rows'), pairs)]
  transfers between devices with their start and end apart: 8 -> 8, of which waited for: 8 -> 4; matrix products, arithmetic and copies ran while one was open for 7% -> 0% of each run, Pallas kernels for 0% -> 22%
where the time goes in v2:
time: 71.1 us; the launch traced here: 70.9 us
  blocking collectives  26.6 us (37%)
  Pallas kernels  19.9 us (28%)
  waiting for transfers between devices  14.3 us (20%)
  starting transfers between devices  8.62 us (12%)
  local copies, waits for them, and re-layouts  1.37 us (2%)
    all_to_all x1, blocking collectives, on_device(): lax.all_to_all(codes.reshape(ROWS, SENT, LANES), 'rows', 0, 0, tiled=True)  26.6 us
    ppermute x8, waiting for transfers between devices, move(): return lax.ppermute(array, ('sparse', 'rows'), pairs)  14.3 us
    pallas_call x4, Pallas kernels, call(): pl.pallas_call(kernel, in_specs=[VMEM] * len(operands), out_specs=VMEM, o...  12.1 us
    ppermute x8, starting transfers between devices, move(): return lax.ppermute(array, ('sparse', 'rows'), pairs)  8.62 us
    pallas_call x1, Pallas kernels, env_unit(): pl.pallas_call(env_kernel, in_specs=[ANY] * (2 + len(after)), out_specs=[...  4.24 us
  transfers between devices with their start and end apart: 8, of which 4 were waited for; matrix products, arithmetic and copies ran while one was open for 0% of the time, Pallas kernels for 22%

profile of v2, /device:TPU:6, one launch (start us, length us, event | category | flops | bytes accessed | tf_op | source)
XLA Modules:
  0.0 70.9 jit_solution(10832706883045036309)
XLA Ops:
  0.0 0.0 collective-permute-start.1
  0.0 1.3 %sparse_unit.1.a = bf16[128,2048]{1,0:T(8,128)(2,1)S(1)} custom-call(bf16[256,2048]{1,0:T(8,128)(2,1)} %desc_ref.1), custom_call_target="tpu_custom_call" | custom-call | flops 1048576 | bytes 1048576 | tf_op jit(solution)/shard_map/sparse_unit/pallas_call | solution.py:97
  1.3 0.9 %collective-permute-start = (bf16[128,2048]{1,0:T(8,128)(2,1)S(1)}, bf16[128,2048]{1,0:T(8,128)(2,1)S(1)}, u32[]{:S(2)}, u32[]{:S(2)}) collective-permute-start(bf16[128,2048]{1,0:T(8,128)(2,1)S(1)} %sparse_unit.1.a), channel_id=1, source_target_pairs={{0,32},{1,35},{2,34},{3,33},{4,36},{5,39},{6,38},{7,37},{8,40},{9,... | collective-permute-start | bytes 1572872 | tf_op jit(solution)/shard_map/ppermute | solution.py:40
  2.2 1.6 %collective-permute-start.2 = (bf16[128,2048]{1,0:T(8,128)(2,1)S(1)}, bf16[128,2048]{1,0:T(8,128)(2,1)S(1)}, u32[]{:S(2)}, u32[]{:S(2)}) collective-permute-start(bf16[128,2048]{1,0:T(8,128)(2,1)S(1)} %sparse_unit.1.a), channel_id=1, source_target_pairs={{0,64},{1,65},{2,66},{3,67},{4,68},{5,69},{6,70},{7,71},{8,72},{9,... | collective-permute-start | bytes 1572872 | tf_op jit(solution)/shard_map/ppermute | solution.py:40
  3.8 1.7 %collective-permute-start.3 = (bf16[128,2048]{1,0:T(8,128)(2,1)S(1)}, bf16[128,2048]{1,0:T(8,128)(2,1)S(1)}, u32[]{:S(2)}, u32[]{:S(2)}) collective-permute-start(bf16[128,2048]{1,0:T(8,128)(2,1)S(1)} %sparse_unit.1.a), channel_id=1, source_target_pairs={{0,192},{1,193},{2,194},{3,195},{4,196},{5,197},{6,198},{7,199},{8... | collective-permute-start | bytes 1572872 | tf_op jit(solution)/shard_map/ppermute | solution.py:40
  5.4 0.0 copy-start
  5.4 0.7 copy-done
  6.1 0.0 copy-start.1
  6.1 0.7 copy-done.1
  6.8 1.1 %book.1 = (bf16[136,1024]{1,0:T(8,128)(2,1)S(1)}, bf16[136,1024]{1,0:T(8,128)(2,1)S(1)}, f32[136,1]{1,0:T(8,128)S(1)}, s32[1,128]{1,0:T(1,128)S(1)}, bf16[64,128...) custom-call(s32[1,1024]{1,0:T(1,128)S(1)} %copy-done, s32[1,1024]{1,0:T(1,128)S(1)} %copy-done.1), custom_call_target="tpu_custom_call" | custom-call | flops 4194304 | bytes 1048576 | tf_op jit(solution)/shard_map/book/pallas_call | solution.py:281
  7.9 2.7 %collective-permute-done.refs_0_.b = bf16[128,2048]{1,0:T(8,128)(2,1)S(1)} collective-permute-done((bf16[128,2048]{1,0:T(8,128)(2,1)S(1)}, bf16[128,2048]{1,0:T(8,128)(2,1)S(1)}, u32[]{:S(2)}, u32[]{:S(2)}) %collective-permute-start) | collective-permute-done | bytes 524320 | tf_op jit(solution)/shard_map/ppermute | solution.py:40
  10.5 0.0 collective-permute-done.1.other_desc
  10.5 4.2 %env_unit.1 = (bf16[1024,2048]{1,0:T(8,128)(2,1)S(1)}, bf16[1024,2048]{1,0:T(8,128)(2,1)S(1)}) custom-call(bf16[1024,2048]{1,0:T(8,128)(2,1)} %own_desc.1, bf16[1024,2048]{1,0:T(8,128)(2,1)S(1)} %collective-permute-done.1.other_desc, bf16[128,2048]{1,0:T(8,128)(2,1)S(1)} %collective-permute-done.refs_0_.b, f32[136,1]{1,0:T(8,128)S(1)} %get-tuple-element.13.refs_1_.inverse), custom_call_target="tpu_custom_call" | custom-call | flops 33554432 | bytes 16777216 | tf_op jit(solution)/shard_map/env_unit/pallas_call | solution.py:133
  14.8 3.0 %early_call.3.refs_0_.sums_0 = f32[136,256]{1,0:T(8,128)S(1)} custom-call(bf16[128,2048]{1,0:T(8,128)(2,1)S(1)} %sparse_unit.1.a, bf16[128,2048]{1,0:T(8,128)(2,1)S(1)} %collective-permute-done.refs_0_.b, bf16[1024,2048]{1,0:T(8,128)(2,1)S(1)} %get-tuple-element.14.own.refs_2_, bf16[1024,2048]{1,0:T(8,128)(2,1)S(1)} %get-tuple-element.15.other.refs_3_, ...), custom_call_target="tpu_custom_call" | custom-call | flops 2147483648 | bytes 8388608 | tf_op jit(solution)/shard_map/early_call/pallas_call | solution.py:374
  17.8 0.0 collective-permute-done.2.a.up_ref
  17.8 0.0 collective-permute-done.3.b.down_ref
  17.8 0.1 choose.1
  17.9 1.7 %collective-permute-start.6 = (bf16[128,2048]{1,0:T(8,128)(2,1)S(1)}, bf16[128,2048]{1,0:T(8,128)(2,1)S(1)}, u32[]{:S(2)}, u32[]{:S(2)}) collective-permute-start(bf16[128,2048]{1,0:T(8,128)(2,1)S(1)} %choose.1), channel_id=1, source_target_pairs={{0,64},{1,193},{2,66},{3,195},{4,68},{5,197},{6,70},{7,199},{8,72}... | collective-permute-start | bytes 1572872 | tf_op jit(solution)/shard_map/ppermute | solution.py:40
  19.5 0.8 %collective-permute-start.4 = (bf16[128,2048]{1,0:T(8,128)(2,1)S(1)}, bf16[128,2048]{1,0:T(8,128)(2,1)S(1)}, u32[]{:S(2)}, u32[]{:S(2)}) collective-permute-start(bf16[128,2048]{1,0:T(8,128)(2,1)S(1)} %collective-permute-done.2.a.up_ref), channel_id=1, source_target_pairs={{0,32},{1,35},{2,34},{3,33},{4,36},{5,39},{6,38},{7,37},{8,40},{9,... | collective-permute-start | bytes 1572872 | tf_op jit(solution)/shard_map/ppermute | solution.py:40
  20.3 1.2 %collective-permute-start.5 = (bf16[128,2048]{1,0:T(8,128)(2,1)S(1)}, bf16[128,2048]{1,0:T(8,128)(2,1)S(1)}, u32[]{:S(2)}, u32[]{:S(2)}) collective-permute-start(bf16[128,2048]{1,0:T(8,128)(2,1)S(1)} %collective-permute-done.3.b.down_ref), channel_id=1, source_target_pairs={{0,32},{1,35},{2,34},{3,33},{4,36},{5,39},{6,38},{7,37},{8,40},{9,... | collective-permute-start | bytes 1572872 | tf_op jit(solution)/shard_map/ppermute | solution.py:40
  21.5 3.0 %early_call.4.refs_0_.sums_1 = f32[136,256]{1,0:T(8,128)S(1)} custom-call(bf16[128,2048]{1,0:T(8,128)(2,1)S(1)} %collective-permute-done.2.a.up_ref, bf16[128,2048]{1,0:T(8,128)(2,1)S(1)} %collective-permute-done.3.b.down_ref, bf16[1024,2048]{1,0:T(8,128)(2,1)S(1)} %get-tuple-element.14.own.refs_2_, bf16[1024,2048]{1,0:T(8,128)(2,1)S(1)} %get-tuple-element.15.other.refs_3_, ...), custom_call_target="tpu_custom_call" | custom-call | flops 2147483648 | bytes 8388608 | tf_op jit(solution)/shard_map/early_call/pallas_call | solution.py:374
  24.5 3.9 %collective-permute-done.6.array_ref.refs_0_ = bf16[128,2048]{1,0:T(8,128)(2,1)S(1)} collective-permute-done((bf16[128,2048]{1,0:T(8,128)(2,1)S(1)}, bf16[128,2048]{1,0:T(8,128)(2,1)S(1)}, u32[]{:S(2)}, u32[]{:S(2)}) %collective-permute-start.6) | collective-permute-done | bytes 524320 | tf_op jit(solution)/shard_map/ppermute | solution.py:40
  28.5 0.8 %collective-permute-start.7 = (bf16[128,2048]{1,0:T(8,128)(2,1)S(1)}, bf16[128,2048]{1,0:T(8,128)(2,1)S(1)}, u32[]{:S(2)}, u32[]{:S(2)}) collective-permute-start(bf16[128,2048]{1,0:T(8,128)(2,1)S(1)} %hold.1), channel_id=1, source_target_pairs={{0,32},{1,35},{2,34},{3,33},{4,36},{5,39},{6,38},{7,37},{8,40},{9,... | collective-permute-start | bytes 1572872 | tf_op jit(solution)/shard_map/ppermute | solution.py:40
  29.3 0.0 collective-permute-done.4.a
  29.3 5.0 %collective-permute-done.5.b = bf16[128,2048]{1,0:T(8,128)(2,1)S(1)} collective-permute-done((bf16[128,2048]{1,0:T(8,128)(2,1)S(1)}, bf16[128,2048]{1,0:T(8,128)(2,1)S(1)}, u32[]{:S(2)}, u32[]{:S(2)}) %collective-permute-start.5) | collective-permute-done | bytes 524320 | tf_op jit(solution)/shard_map/ppermute | solution.py:40
  34.3 3.0 %early_call.5.sums_2 = f32[136,256]{1,0:T(8,128)S(1)} custom-call(bf16[128,2048]{1,0:T(8,128)(2,1)S(1)} %collective-permute-done.4.a, bf16[128,2048]{1,0:T(8,128)(2,1)S(1)} %collective-permute-done.5.b, bf16[1024,2048]{1,0:T(8,128)(2,1)S(1)} %get-tuple-element.14.own.refs_2_, bf16[1024,2048]{1,0:T(8,128)(2,1)S(1)} %get-tuple-element.15.other.refs_3_, ...), custom_call_target="tpu_custom_call" | custom-call | flops 2147483648 | bytes 8388608 | tf_op jit(solution)/shard_map/early_call/pallas_call | solution.py:374
  37.3 2.6 %collective-permute-done.7.refs_1_ = bf16[128,2048]{1,0:T(8,128)(2,1)S(1)} collective-permute-done((bf16[128,2048]{1,0:T(8,128)(2,1)S(1)}, bf16[128,2048]{1,0:T(8,128)(2,1)S(1)}, u32[]{:S(2)}, u32[]{:S(2)}) %collective-permute-start.7) | collective-permute-done | bytes 524320 | tf_op jit(solution)/shard_map/ppermute | solution.py:40
  39.9 3.1 %last_call.1 = s16[16,80,128]{2,1,0:T(8,128)(2,1)S(1)} custom-call(f32[136,256]{1,0:T(8,128)S(1)} %early_call.3.refs_0_.sums_0, f32[136,256]{1,0:T(8,128)S(1)} %early_call.4.refs_0_.sums_1, f32[136,256]{1,0:T(8,128)S(1)} %early_call.5.sums_2, f32[136,1]{1,0:T(8,128)S(1)} %get-tuple-element.13.refs_1_.inverse, s32[1,128]{1,0:T(1,128)S(1)} %get-tuple-element.18.more_owner, ...), custom_call_target="tpu_custom_call" | custom-call | flops 2147483648 | bytes 8388608 | tf_op jit(solution)/shard_map/last_call/pallas_call | solution.py:374
  43.1 26.6 %all_to_all.5 = s16[32,40,128]{2,1,0:T(8,128)(2,1)S(1)} all-to-all(s16[32,40,128]{2,1,0:T(8,128)(2,1)S(1)} %bitcast.2), channel_id=1, replica_groups=mesh['sparse'=8,'rows'=32] {'rows'}, dimensions={0} | all-to-all | bytes 655360 | tf_op jit(solution)/shard_map/all_to_all | solution.py:454
  69.6 1.2 %combine.1 = f32[32,2048]{1,0:T(8,128)} custom-call(s16[16,80,128]{2,1,0:T(8,128)(2,1)S(1)} %bitcast.3, bf16[64,128]{1,0:T(8,128)(2,1)S(1)} %get-tuple-element.19.pick_ref, bf16[256,128]{1,0:T(8,128)(2,1)S(1)} %get-tuple-element.20.pick_more_ref), custom_call_target="tpu_custom_call" | custom-call | tf_op jit(solution)/shard_map/combine/pallas_call | solution.py:420
  (1 shorter events, 0.0 us)
Async XLA Ops:
  0.0 10.5 %collective-permute-start.1 = (bf16[1024,2048]{1,0:T(8,128)(2,1)}, bf16[1024,2048]{1,0:T(8,128)(2,1)S(1)}, u32[]{:S(2)}, u32[]{:S(2)}) collective-permute-start(bf16[1024,2048]{1,0:T(8,128)(2,1)} %own_desc.1), channel_id=1, source_target_pairs={{0,1},{1,0},{2,3},{3,2},{4,5},{5,4},{6,7},{7,6},{8,9},{9,8},{10,11... | collective-permute-start | bytes 12582920 | tf_op jit(solution)/shard_map/ppermute | solution.py:40
  1.3 9.3 %collective-permute-start = (bf16[128,2048]{1,0:T(8,128)(2,1)S(1)}, bf16[128,2048]{1,0:T(8,128)(2,1)S(1)}, u32[]{:S(2)}, u32[]{:S(2)}) collective-permute-start(bf16[128,2048]{1,0:T(8,128)(2,1)S(1)} %sparse_unit.1.a), channel_id=1, source_target_pairs={{0,32},{1,35},{2,34},{3,33},{4,36},{5,39},{6,38},{7,37},{8,40},{9,... | collective-permute-start | bytes 1572872 | tf_op jit(solution)/shard_map/ppermute | solution.py:40
  2.2 15.6 %collective-permute-start.2 = (bf16[128,2048]{1,0:T(8,128)(2,1)S(1)}, bf16[128,2048]{1,0:T(8,128)(2,1)S(1)}, u32[]{:S(2)}, u32[]{:S(2)}) collective-permute-start(bf16[128,2048]{1,0:T(8,128)(2,1)S(1)} %sparse_unit.1.a), channel_id=1, source_target_pairs={{0,64},{1,65},{2,66},{3,67},{4,68},{5,69},{6,70},{7,71},{8,72},{9,... | collective-permute-start | bytes 1572872 | tf_op jit(solution)/shard_map/ppermute | solution.py:40
  3.8 14.0 %collective-permute-start.3 = (bf16[128,2048]{1,0:T(8,128)(2,1)S(1)}, bf16[128,2048]{1,0:T(8,128)(2,1)S(1)}, u32[]{:S(2)}, u32[]{:S(2)}) collective-permute-start(bf16[128,2048]{1,0:T(8,128)(2,1)S(1)} %sparse_unit.1.a), channel_id=1, source_target_pairs={{0,192},{1,193},{2,194},{3,195},{4,196},{5,197},{6,198},{7,199},{8... | collective-permute-start | bytes 1572872 | tf_op jit(solution)/shard_map/ppermute | solution.py:40
  5.4 0.7 copy-start
  6.1 0.7 copy-start.1
  17.9 10.6 %collective-permute-start.6 = (bf16[128,2048]{1,0:T(8,128)(2,1)S(1)}, bf16[128,2048]{1,0:T(8,128)(2,1)S(1)}, u32[]{:S(2)}, u32[]{:S(2)}) collective-permute-start(bf16[128,2048]{1,0:T(8,128)(2,1)S(1)} %choose.1), channel_id=1, source_target_pairs={{0,64},{1,193},{2,66},{3,195},{4,68},{5,197},{6,70},{7,199},{8,72}... | collective-permute-start | bytes 1572872 | tf_op jit(solution)/shard_map/ppermute | solution.py:40
  19.5 9.8 %collective-permute-start.4 = (bf16[128,2048]{1,0:T(8,128)(2,1)S(1)}, bf16[128,2048]{1,0:T(8,128)(2,1)S(1)}, u32[]{:S(2)}, u32[]{:S(2)}) collective-permute-start(bf16[128,2048]{1,0:T(8,128)(2,1)S(1)} %collective-permute-done.2.a.up_ref), channel_id=1, source_target_pairs={{0,32},{1,35},{2,34},{3,33},{4,36},{5,39},{6,38},{7,37},{8,40},{9,... | collective-permute-start | bytes 1572872 | tf_op jit(solution)/shard_map/ppermute | solution.py:40
  20.3 14.0 %collective-permute-start.5 = (bf16[128,2048]{1,0:T(8,128)(2,1)S(1)}, bf16[128,2048]{1,0:T(8,128)(2,1)S(1)}, u32[]{:S(2)}, u32[]{:S(2)}) collective-permute-start(bf16[128,2048]{1,0:T(8,128)(2,1)S(1)} %collective-permute-done.3.b.down_ref), channel_id=1, source_target_pairs={{0,32},{1,35},{2,34},{3,33},{4,36},{5,39},{6,38},{7,37},{8,40},{9,... | collective-permute-start | bytes 1572872 | tf_op jit(solution)/shard_map/ppermute | solution.py:40
  28.5 11.4 %collective-permute-start.7 = (bf16[128,2048]{1,0:T(8,128)(2,1)S(1)}, bf16[128,2048]{1,0:T(8,128)(2,1)S(1)}, u32[]{:S(2)}, u32[]{:S(2)}) collective-permute-start(bf16[128,2048]{1,0:T(8,128)(2,1)S(1)} %hold.1), channel_id=1, source_target_pairs={{0,32},{1,35},{2,34},{3,33},{4,36},{5,39},{6,38},{7,37},{8,40},{9,... | collective-permute-start | bytes 1572872 | tf_op jit(solution)/shard_map/ppermute | solution.py:40

commit v3 on v2

--- a/solution.py
+++ b/solution.py
@@ -54,6 +54,10 @@
 
 def onward(y, xl, z, xh, core):
     return (y + 1 if core == 0 else y - 1), xl, z, xh, core
+
+
+def opposite(y, xl, z, xh, core):
+    return y + 2, xl, z, xh, core
 
 
 def other_core(y, xl, z, xh, core):
@@ -162,19 +166,20 @@
     )(from_up, from_down, *after)
 
 
-def hold_kernel(array_ref, *refs):
-    refs[-1][...] = array_ref[...]
-
-
-def hold(array, after):
-    return pl.pallas_call(
-        hold_kernel,
+def rows_kernel(array_ref, *refs, begin):
+    refs[-1][...] = array_ref[begin : begin + refs[-1].shape[0]]
+
+
+def rows_of(array, begin, count, after):
+    width = array.shape[1]
+    return pl.pallas_call(
+        functools.partial(rows_kernel, begin=begin),
         in_specs=[VMEM] + [ANY] * len(after),
         out_specs=VMEM,
-        out_shape=jax.ShapeDtypeStruct(array.shape, array.dtype),
+        out_shape=jax.ShapeDtypeStruct((count, width), array.dtype),
         compiler_params=params(4),
-        cost_estimate=cost(0, 4 * array.size),
-        name="hold",
+        cost_estimate=cost(0, 4 * count * width),
+        name="rows_of",
     )(array, *after)
 
 
@@ -304,10 +309,12 @@
     return high, (kernel - high.astype(jnp.float32)).astype(jnp.bfloat16)
 
 
-def block_sums(a, b, own, other, of_own, of_other, block, high, low):
-    half = a.shape[0]
-    block[:half] = a[...]
-    block[half:] = b[...]
+def block_sums(*refs):
+    *pieces, own, other, of_own, of_other, block, high, low = refs
+    at = 0
+    for piece in pieces:
+        block[at : at + piece.shape[0]] = piece[...]
+        at += piece.shape[0]
     rows = own.shape[0]
     tile = 512
     for begin, env in ((0, own), (rows, other)):
@@ -344,7 +351,9 @@
 def last_call(sums_0, sums_1, sums_2, inverse, more_owner, *refs):
     *operands, out_ref, block, high, low = refs
     last = block_sums(*operands, block, high, low)
-    means = [part * inverse[...] for part in (sums_0[...], sums_1[...], sums_2[...], last)]
+    near = jnp.concatenate([sums_2[:, :LANES], last[:, :LANES]], axis=1)
+    far = jnp.concatenate([sums_2[:, LANES:], last[:, LANES:]], axis=1)
+    means = [part * inverse[...] for part in (sums_0[...], sums_1[...], near, far)]
     tiles = (ROWS // 2, 2 * KEEP, LANES)
     lower = lax.broadcasted_iota(jnp.int32, tiles, 1) < KEEP
     owner = 2 * lax.broadcasted_iota(jnp.int32, tiles, 0)
@@ -439,14 +448,19 @@
     sums = jax.ShapeDtypeStruct((HELD_ROWS, 2 * LANES), jnp.float32)
     sums_0 = call(early_call, (), (half, near), envs, members, sums)
     far = move(choose(from_up, from_down, (sums_0,)), onward)
-    near_up, near_down = move(from_up, across), move(from_down, across)
+    near_up = move(from_up, across)
     sums_1 = call(early_call, (), (from_up, from_down), envs, members, sums)
-    near_far = move(hold(far, (sums_1,)), across)
-    sums_2 = call(early_call, (), (near_up, near_down), envs, members, sums)
+    after = (sums_1,)
+    count = half.shape[0]
+    near_down = move(rows_of(from_down, 0, count, after), across)
+    by_y = count // 16 * 3 // 8 * 16
+    near_far_a = move(rows_of(near, 0, by_y, (far, *after)), opposite)
+    near_far_b = move(rows_of(far, by_y, count - by_y, after), across)
+    sums_2 = call(early_call, (), (near_up, far), envs, members, sums)
     codes = call(
         last_call,
         (sums_0, sums_1, sums_2, inverse, more_owner),
-        (far, near_far),
+        (near_down, near_far_a, near_far_b),
         envs,
         members,
         jax.ShapeDtypeStruct((ROWS // 2, 2 * SENT, LANES), jnp.int16),

time: 71.1 us -> 69 us (0.970)
  waiting for transfers between devices: 14.3 us -> 9.95 us
  starting transfers between devices: 8.62 us -> 10.8 us
    ppermute x8 -> x9, waiting for transfers between devices: 14.3 us -> 9.95 us  [move(): return lax.ppermute(array, ('sparse', 'rows'), pairs)]
    ppermute x8 -> x9, starting transfers between devices: 8.62 us -> 10.8 us  [move(): return lax.ppermute(array, ('sparse', 'rows'), pairs)]
  transfers between devices with their start and end apart: 8 -> 9, of which waited for: 4 -> 4; matrix products, arithmetic and copies ran while one was open for 0% -> 0% of each run, Pallas kernels for 22% -> 23%
where the time goes in v3:
time: 69 us; the launch traced here: 68.8 us
  blocking collectives  26.6 us (39%)
  Pallas kernels  20 us (29%)
  starting transfers between devices  10.8 us (16%)
  waiting for transfers between devices  9.95 us (14%)
  local copies, waits for them, and re-layouts  1.37 us (2%)
    all_to_all x1, blocking collectives, on_device(): lax.all_to_all(codes.reshape(ROWS, SENT, LANES), 'rows', 0, 0, tiled=True)  26.6 us
    pallas_call x4, Pallas kernels, call(): pl.pallas_call(kernel, in_specs=[VMEM] * len(operands), out_specs=VMEM, o...  12.1 us
    ppermute x9, starting transfers between devices, move(): return lax.ppermute(array, ('sparse', 'rows'), pairs)  10.8 us
    ppermute x9, waiting for transfers between devices, move(): return lax.ppermute(array, ('sparse', 'rows'), pairs)  9.95 us
    pallas_call x1, Pallas kernels, env_unit(): pl.pallas_call(env_kernel, in_specs=[ANY] * (2 + len(after)), out_specs=[...  4.24 us
  transfers between devices with their start and end apart: 9, of which 4 were waited for; matrix products, arithmetic and copies ran while one was open for 0% of the time, Pallas kernels for 23%

profile of v3, /device:TPU:6, one launch (start us, length us, event | category | flops | bytes accessed | tf_op | source)
XLA Modules:
  0.0 68.8 jit_solution(69068024050703136)
XLA Ops:
  0.0 0.0 collective-permute-start.1
  0.0 1.3 %sparse_unit.1.a = bf16[128,2048]{1,0:T(8,128)(2,1)S(1)} custom-call(bf16[256,2048]{1,0:T(8,128)(2,1)} %desc_ref.1), custom_call_target="tpu_custom_call" | custom-call | flops 1048576 | bytes 1048576 | tf_op jit(solution)/shard_map/sparse_unit/pallas_call | solution.py:101
  1.3 0.9 %collective-permute-start = (bf16[128,2048]{1,0:T(8,128)(2,1)S(1)}, bf16[128,2048]{1,0:T(8,128)(2,1)S(1)}, u32[]{:S(2)}, u32[]{:S(2)}) collective-permute-start(bf16[128,2048]{1,0:T(8,128)(2,1)S(1)} %sparse_unit.1.a), channel_id=1, source_target_pairs={{0,32},{1,35},{2,34},{3,33},{4,36},{5,39},{6,38},{7,37},{8,40},{9,... | collective-permute-start | bytes 1572872 | tf_op jit(solution)/shard_map/ppermute | solution.py:40
  2.2 1.6 %collective-permute-start.2 = (bf16[128,2048]{1,0:T(8,128)(2,1)S(1)}, bf16[128,2048]{1,0:T(8,128)(2,1)S(1)}, u32[]{:S(2)}, u32[]{:S(2)}) collective-permute-start(bf16[128,2048]{1,0:T(8,128)(2,1)S(1)} %sparse_unit.1.a), channel_id=1, source_target_pairs={{0,64},{1,65},{2,66},{3,67},{4,68},{5,69},{6,70},{7,71},{8,72},{9,... | collective-permute-start | bytes 1572872 | tf_op jit(solution)/shard_map/ppermute | solution.py:40
  3.8 1.7 %collective-permute-start.3 = (bf16[128,2048]{1,0:T(8,128)(2,1)S(1)}, bf16[128,2048]{1,0:T(8,128)(2,1)S(1)}, u32[]{:S(2)}, u32[]{:S(2)}) collective-permute-start(bf16[128,2048]{1,0:T(8,128)(2,1)S(1)} %sparse_unit.1.a), channel_id=1, source_target_pairs={{0,192},{1,193},{2,194},{3,195},{4,196},{5,197},{6,198},{7,199},{8... | collective-permute-start | bytes 1572872 | tf_op jit(solution)/shard_map/ppermute | solution.py:40
  5.4 0.0 copy-start
  5.4 0.7 copy-done
  6.1 0.0 copy-start.1
  6.1 0.7 copy-done.1
  6.8 1.1 %book.1 = (bf16[136,1024]{1,0:T(8,128)(2,1)S(1)}, bf16[136,1024]{1,0:T(8,128)(2,1)S(1)}, f32[136,1]{1,0:T(8,128)S(1)}, s32[1,128]{1,0:T(1,128)S(1)}, bf16[64,128...) custom-call(s32[1,1024]{1,0:T(1,128)S(1)} %copy-done, s32[1,1024]{1,0:T(1,128)S(1)} %copy-done.1), custom_call_target="tpu_custom_call" | custom-call | flops 4194304 | bytes 1048576 | tf_op jit(solution)/shard_map/book/pallas_call | solution.py:286
  7.9 2.7 %collective-permute-done.refs_0_.b.array_ref = bf16[128,2048]{1,0:T(8,128)(2,1)S(1)} collective-permute-done((bf16[128,2048]{1,0:T(8,128)(2,1)S(1)}, bf16[128,2048]{1,0:T(8,128)(2,1)S(1)}, u32[]{:S(2)}, u32[]{:S(2)}) %collective-permute-start) | collective-permute-done | bytes 524320 | tf_op jit(solution)/shard_map/ppermute | solution.py:40
  10.5 0.0 collective-permute-done.1.other_desc
  10.5 4.2 %env_unit.1 = (bf16[1024,2048]{1,0:T(8,128)(2,1)S(1)}, bf16[1024,2048]{1,0:T(8,128)(2,1)S(1)}) custom-call(bf16[1024,2048]{1,0:T(8,128)(2,1)} %own_desc.1, bf16[1024,2048]{1,0:T(8,128)(2,1)S(1)} %collective-permute-done.1.other_desc, bf16[128,2048]{1,0:T(8,128)(2,1)S(1)} %collective-permute-done.refs_0_.b.array_ref, ...), custom_call_target="tpu_custom_call" | custom-call | flops 33554432 | bytes 16777216 | tf_op jit(solution)/shard_map/env_unit/pallas_call | solution.py:137
  14.8 3.0 %early_call.3.refs_0_.sums_0 = f32[136,256]{1,0:T(8,128)S(1)} custom-call(bf16[128,2048]{1,0:T(8,128)(2,1)S(1)} %sparse_unit.1.a, bf16[128,2048]{1,0:T(8,128)(2,1)S(1)} %collective-permute-done.refs_0_.b.array_ref, bf16[1024,2048]{1,0:T(8,128)(2,1)S(1)} %get-tuple-element.14.own.refs_3_, bf16[1024,2048]{1,0:T(8,128)(2,1)S(1)} %get-tuple-element.15.other.refs_4_, ...), custom_call_target="tpu_custom_call" | custom-call | flops 2147483648 | bytes 8388608 | tf_op jit(solution)/shard_map/early_call/pallas_call | solution.py:383
  17.8 0.0 collective-permute-done.2.a.up_ref
  17.8 0.0 collective-permute-done.3.b.down_ref.array_ref
  17.8 0.1 choose.1
  17.9 1.7 %collective-permute-start.5 = (bf16[128,2048]{1,0:T(8,128)(2,1)S(1)}, bf16[128,2048]{1,0:T(8,128)(2,1)S(1)}, u32[]{:S(2)}, u32[]{:S(2)}) collective-permute-start(bf16[128,2048]{1,0:T(8,128)(2,1)S(1)} %choose.1), channel_id=1, source_target_pairs={{0,64},{1,193},{2,66},{3,195},{4,68},{5,197},{6,70},{7,199},{8,72}... | collective-permute-start | bytes 1572872 | tf_op jit(solution)/shard_map/ppermute | solution.py:40
  19.5 0.8 %collective-permute-start.4 = (bf16[128,2048]{1,0:T(8,128)(2,1)S(1)}, bf16[128,2048]{1,0:T(8,128)(2,1)S(1)}, u32[]{:S(2)}, u32[]{:S(2)}) collective-permute-start(bf16[128,2048]{1,0:T(8,128)(2,1)S(1)} %collective-permute-done.2.a.up_ref), channel_id=1, source_target_pairs={{0,32},{1,35},{2,34},{3,33},{4,36},{5,39},{6,38},{7,37},{8,40},{9,... | collective-permute-start | bytes 1572872 | tf_op jit(solution)/shard_map/ppermute | solution.py:40
  20.4 3.0 %early_call.4.refs_0_.refs_1_.sums_1 = f32[136,256]{1,0:T(8,128)S(1)} custom-call(bf16[128,2048]{1,0:T(8,128)(2,1)S(1)} %collective-permute-done.2.a.up_ref, bf16[128,2048]{1,0:T(8,128)(2,1)S(1)} %collective-permute-done.3.b.down_ref.array_ref, bf16[1024,2048]{1,0:T(8,128)(2,1)S(1)} %get-tuple-element.14.own.refs_3_, ...), custom_call_target="tpu_custom_call" | custom-call | flops 2147483648 | bytes 8388608 | tf_op jit(solution)/shard_map/early_call/pallas_call | solution.py:383
  23.4 1.3 %collective-permute-start.6 = (bf16[128,2048]{1,0:T(8,128)(2,1)S(1)}, bf16[128,2048]{1,0:T(8,128)(2,1)S(1)}, u32[]{:S(2)}, u32[]{:S(2)}) collective-permute-start(bf16[128,2048]{1,0:T(8,128)(2,1)S(1)} %rows_of.3), channel_id=1, source_target_pairs={{0,32},{1,35},{2,34},{3,33},{4,36},{5,39},{6,38},{7,37},{8,40},{9,... | collective-permute-start | bytes 1572872 | tf_op jit(solution)/shard_map/ppermute | solution.py:40
  24.7 3.8 %collective-permute-done.5.b.refs_0_.array_ref = bf16[128,2048]{1,0:T(8,128)(2,1)S(1)} collective-permute-done((bf16[128,2048]{1,0:T(8,128)(2,1)S(1)}, bf16[128,2048]{1,0:T(8,128)(2,1)S(1)}, u32[]{:S(2)}, u32[]{:S(2)}) %collective-permute-start.5) | collective-permute-done | bytes 524320 | tf_op jit(solution)/shard_map/ppermute | solution.py:40
  28.5 0.8 %collective-permute-start.8 = (bf16[80,2048]{1,0:T(8,128)(2,1)S(1)}, bf16[80,2048]{1,0:T(8,128)(2,1)S(1)}, u32[]{:S(2)}, u32[]{:S(2)}) collective-permute-start(bf16[80,2048]{1,0:T(8,128)(2,1)S(1)} %rows_of.5), channel_id=1, source_target_pairs={{0,32},{1,35},{2,34},{3,33},{4,36},{5,39},{6,38},{7,37},{8,40},{9,... | collective-permute-start | bytes 983048 | tf_op jit(solution)/shard_map/ppermute | solution.py:40
  29.3 2.1 %collective-permute-start.7 = (bf16[48,2048]{1,0:T(8,128)(2,1)S(1)}, bf16[48,2048]{1,0:T(8,128)(2,1)S(1)}, u32[]{:S(2)}, u32[]{:S(2)}) collective-permute-start(bf16[48,2048]{1,0:T(8,128)(2,1)S(1)} %rows_of.4), channel_id=1, source_target_pairs={{0,128},{1,129},{2,130},{3,131},{4,132},{5,133},{6,134},{7,135},{8... | collective-permute-start | bytes 589832 | tf_op jit(solution)/shard_map/ppermute | solution.py:40
  31.4 0.0 collective-permute-done.4.a
  31.4 3.0 %early_call.5.sums_2 = f32[136,256]{1,0:T(8,128)S(1)} custom-call(bf16[128,2048]{1,0:T(8,128)(2,1)S(1)} %collective-permute-done.4.a, bf16[128,2048]{1,0:T(8,128)(2,1)S(1)} %collective-permute-done.5.b.refs_0_.array_ref, bf16[1024,2048]{1,0:T(8,128)(2,1)S(1)} %get-tuple-element.14.own.refs_3_, bf16[1024,2048]{1,0:T(8,128)(2,1)S(1)} %get-tuple-element.15.other.refs_4_, ...), custom_call_target="tpu_custom_call" | custom-call | flops 2147483648 | bytes 8388608 | tf_op jit(solution)/shard_map/early_call/pallas_call | solution.py:383
  34.4 0.0 collective-permute-done.6.refs_0_
  34.4 3.2 %collective-permute-done.7.refs_1_ = bf16[48,2048]{1,0:T(8,128)(2,1)S(1)} collective-permute-done((bf16[48,2048]{1,0:T(8,128)(2,1)S(1)}, bf16[48,2048]{1,0:T(8,128)(2,1)S(1)}, u32[]{:S(2)}, u32[]{:S(2)}) %collective-permute-start.7) | collective-permute-done | bytes 196640 | tf_op jit(solution)/shard_map/ppermute | solution.py:40
  37.6 0.2 collective-permute-done.8.refs_2_
  37.8 3.1 %last_call.1 = s16[16,80,128]{2,1,0:T(8,128)(2,1)S(1)} custom-call(f32[136,256]{1,0:T(8,128)S(1)} %early_call.3.refs_0_.sums_0, f32[136,256]{1,0:T(8,128)S(1)} %early_call.4.refs_0_.refs_1_.sums_1, f32[136,256]{1,0:T(8,128)S(1)} %early_call.5.sums_2, f32[136,1]{1,0:T(8,128)S(1)} %get-tuple-element.13.refs_1_.inverse, ...), custom_call_target="tpu_custom_call" | custom-call | flops 2147483648 | bytes 8388608 | tf_op jit(solution)/shard_map/last_call/pallas_call | solution.py:383
  41.0 26.6 %all_to_all.5 = s16[32,40,128]{2,1,0:T(8,128)(2,1)S(1)} all-to-all(s16[32,40,128]{2,1,0:T(8,128)(2,1)S(1)} %bitcast.2), channel_id=1, replica_groups=mesh['sparse'=8,'rows'=32] {'rows'}, dimensions={0} | all-to-all | bytes 655360 | tf_op jit(solution)/shard_map/all_to_all | solution.py:468
  67.5 1.2 %combine.1 = f32[32,2048]{1,0:T(8,128)} custom-call(s16[16,80,128]{2,1,0:T(8,128)(2,1)S(1)} %bitcast.3, bf16[64,128]{1,0:T(8,128)(2,1)S(1)} %get-tuple-element.19.pick_ref, bf16[256,128]{1,0:T(8,128)(2,1)S(1)} %get-tuple-element.20.pick_more_ref), custom_call_target="tpu_custom_call" | custom-call | tf_op jit(solution)/shard_map/combine/pallas_call | solution.py:429
  (3 shorter events, 0.1 us)
Async XLA Ops:
  0.0 10.5 %collective-permute-start.1 = (bf16[1024,2048]{1,0:T(8,128)(2,1)}, bf16[1024,2048]{1,0:T(8,128)(2,1)S(1)}, u32[]{:S(2)}, u32[]{:S(2)}) collective-permute-start(bf16[1024,2048]{1,0:T(8,128)(2,1)} %own_desc.1), channel_id=1, source_target_pairs={{0,1},{1,0},{2,3},{3,2},{4,5},{5,4},{6,7},{7,6},{8,9},{9,8},{10,11... | collective-permute-start | bytes 12582920 | tf_op jit(solution)/shard_map/ppermute | solution.py:40
  1.3 9.3 %collective-permute-start = (bf16[128,2048]{1,0:T(8,128)(2,1)S(1)}, bf16[128,2048]{1,0:T(8,128)(2,1)S(1)}, u32[]{:S(2)}, u32[]{:S(2)}) collective-permute-start(bf16[128,2048]{1,0:T(8,128)(2,1)S(1)} %sparse_unit.1.a), channel_id=1, source_target_pairs={{0,32},{1,35},{2,34},{3,33},{4,36},{5,39},{6,38},{7,37},{8,40},{9,... | collective-permute-start | bytes 1572872 | tf_op jit(solution)/shard_map/ppermute | solution.py:40
  2.2 15.6 %collective-permute-start.2 = (bf16[128,2048]{1,0:T(8,128)(2,1)S(1)}, bf16[128,2048]{1,0:T(8,128)(2,1)S(1)}, u32[]{:S(2)}, u32[]{:S(2)}) collective-permute-start(bf16[128,2048]{1,0:T(8,128)(2,1)S(1)} %sparse_unit.1.a), channel_id=1, source_target_pairs={{0,64},{1,65},{2,66},{3,67},{4,68},{5,69},{6,70},{7,71},{8,72},{9,... | collective-permute-start | bytes 1572872 | tf_op jit(solution)/shard_map/ppermute | solution.py:40
  3.8 14.0 %collective-permute-start.3 = (bf16[128,2048]{1,0:T(8,128)(2,1)S(1)}, bf16[128,2048]{1,0:T(8,128)(2,1)S(1)}, u32[]{:S(2)}, u32[]{:S(2)}) collective-permute-start(bf16[128,2048]{1,0:T(8,128)(2,1)S(1)} %sparse_unit.1.a), channel_id=1, source_target_pairs={{0,192},{1,193},{2,194},{3,195},{4,196},{5,197},{6,198},{7,199},{8... | collective-permute-start | bytes 1572872 | tf_op jit(solution)/shard_map/ppermute | solution.py:40
  5.4 0.7 copy-start
  6.1 0.7 copy-start.1
  17.9 10.6 %collective-permute-start.5 = (bf16[128,2048]{1,0:T(8,128)(2,1)S(1)}, bf16[128,2048]{1,0:T(8,128)(2,1)S(1)}, u32[]{:S(2)}, u32[]{:S(2)}) collective-permute-start(bf16[128,2048]{1,0:T(8,128)(2,1)S(1)} %choose.1), channel_id=1, source_target_pairs={{0,64},{1,193},{2,66},{3,195},{4,68},{5,197},{6,70},{7,199},{8,72}... | collective-permute-start | bytes 1572872 | tf_op jit(solution)/shard_map/ppermute | solution.py:40
  19.5 11.8 %collective-permute-start.4 = (bf16[128,2048]{1,0:T(8,128)(2,1)S(1)}, bf16[128,2048]{1,0:T(8,128)(2,1)S(1)}, u32[]{:S(2)}, u32[]{:S(2)}) collective-permute-start(bf16[128,2048]{1,0:T(8,128)(2,1)S(1)} %collective-permute-done.2.a.up_ref), channel_id=1, source_target_pairs={{0,32},{1,35},{2,34},{3,33},{4,36},{5,39},{6,38},{7,37},{8,40},{9,... | collective-permute-start | bytes 1572872 | tf_op jit(solution)/shard_map/ppermute | solution.py:40
  23.4 11.0 %collective-permute-start.6 = (bf16[128,2048]{1,0:T(8,128)(2,1)S(1)}, bf16[128,2048]{1,0:T(8,128)(2,1)S(1)}, u32[]{:S(2)}, u32[]{:S(2)}) collective-permute-start(bf16[128,2048]{1,0:T(8,128)(2,1)S(1)} %rows_of.3), channel_id=1, source_target_pairs={{0,32},{1,35},{2,34},{3,33},{4,36},{5,39},{6,38},{7,37},{8,40},{9,... | collective-permute-start | bytes 1572872 | tf_op jit(solution)/shard_map/ppermute | solution.py:40
  28.5 9.3 %collective-permute-start.8 = (bf16[80,2048]{1,0:T(8,128)(2,1)S(1)}, bf16[80,2048]{1,0:T(8,128)(2,1)S(1)}, u32[]{:S(2)}, u32[]{:S(2)}) collective-permute-start(bf16[80,2048]{1,0:T(8,128)(2,1)S(1)} %rows_of.5), channel_id=1, source_target_pairs={{0,32},{1,35},{2,34},{3,33},{4,36},{5,39},{6,38},{7,37},{8,40},{9,... | collective-permute-start | bytes 983048 | tf_op jit(solution)/shard_map/ppermute | solution.py:40
  29.3 8.3 %collective-permute-start.7 = (bf16[48,2048]{1,0:T(8,128)(2,1)S(1)}, bf16[48,2048]{1,0:T(8,128)(2,1)S(1)}, u32[]{:S(2)}, u32[]{:S(2)}) collective-permute-start(bf16[48,2048]{1,0:T(8,128)(2,1)S(1)} %rows_of.4), channel_id=1, source_target_pairs={{0,128},{1,129},{2,130},{3,131},{4,132},{5,133},{6,134},{7,135},{8... | collective-permute-start | bytes 589832 | tf_op jit(solution)/shard_map/ppermute | solution.py:40

commit v4 on v3

--- a/solution.py
+++ b/solution.py
@@ -16,7 +16,7 @@
 SENT = 8 * KEEP + 8
 LANES = 128
 MIB = 1 << 20
-SHIFTS = ((0, 0), (0, 1), (3, 0), (1, 0), (3, 1), (1, 1), (2, 0), (2, 1))
+SHIFTS = ((0, 0), (0, 1), (3, 0), (1, 0), (3, 1), (2, 0), (1, 1), (2, 1))
 STEPS, LEAST, ZERO = 512.0, 126.0, 32768
 
 VMEM = pl.BlockSpec(memory_space=pltpu.VMEM)
@@ -40,14 +40,6 @@
     return lax.ppermute(array, ("sparse", "rows"), pairs)
 
 
-def up(y, xl, z, xh, core):
-    return y + 1, xl, z, xh, core
-
-
-def down(y, xl, z, xh, core):
-    return y - 1, xl, z, xh, core
-
-
 def across(y, xl, z, xh, core):
     return y, 1 - xl, z, (xh + core) % XH, core
 
@@ -58,6 +50,10 @@
 
 def opposite(y, xl, z, xh, core):
     return y + 2, xl, z, xh, core
+
+
+def back(y, xl, z, xh, core):
+    return (y - 1 if core == 0 else y + 1), xl, z, xh, core
 
 
 def other_core(y, xl, z, xh, core):
@@ -147,23 +143,6 @@
         cost_estimate=cost(16 * rows * width, 8 * rows * width),
         name="env_unit",
     )(in_hbm(own), other, *after)
-
-
-def choose_kernel(up_ref, down_ref, *refs):
-    first = lax.axis_index("rows") % CORE == 0
-    refs[-1][...] = jnp.where(first, up_ref[...], down_ref[...])
-
-
-def choose(from_up, from_down, after):
-    return pl.pallas_call(
-        choose_kernel,
-        in_specs=[VMEM, VMEM] + [ANY] * len(after),
-        out_specs=VMEM,
-        out_shape=jax.ShapeDtypeStruct(from_up.shape, from_up.dtype),
-        compiler_params=params(4),
-        cost_estimate=cost(0, 6 * from_up.size),
-        name="choose",
-    )(from_up, from_down, *after)
 
 
 def rows_kernel(array_ref, *refs, begin):
@@ -338,7 +317,7 @@
 
 
 def encode(sums):
-    position = (jnp.log2(jnp.maximum(sums, 1e-37)) + LEAST) * STEPS
+    position = (jnp.log2(jnp.maximum(sums, 2.0**-126)) + LEAST) * STEPS
     code = jnp.clip(jnp.round(position), 0.0, 65534.0).astype(jnp.int32) + (1 - ZERO)
     return jnp.where(sums >= 2.0**-126, code, -ZERO)
 
@@ -351,9 +330,7 @@
 def last_call(sums_0, sums_1, sums_2, inverse, more_owner, *refs):
     *operands, out_ref, block, high, low = refs
     last = block_sums(*operands, block, high, low)
-    near = jnp.concatenate([sums_2[:, :LANES], last[:, :LANES]], axis=1)
-    far = jnp.concatenate([sums_2[:, LANES:], last[:, LANES:]], axis=1)
-    means = [part * inverse[...] for part in (sums_0[...], sums_1[...], near, far)]
+    means = [part * inverse[...] for part in (sums_0[...], sums_1[...], sums_2[...], last)]
     tiles = (ROWS // 2, 2 * KEEP, LANES)
     lower = lax.broadcasted_iota(jnp.int32, tiles, 1) < KEEP
     owner = 2 * lax.broadcasted_iota(jnp.int32, tiles, 0)
@@ -420,6 +397,7 @@
             sums = picked(pick_ref[...], tile) + more[2 * i * count : 2 * (i + 1) * count]
             for half in range(2):
                 dy, dx = SHIFTS[2 * i + half]
+                dy = dy if core == 0 else Y - dy
                 column = ((y + dy) % Y * XL + (xl + dx) % XL) * CORE + core
                 at = pl.multiple_of(column * LANES, LANES)
                 out_ref[:, pl.ds(at, LANES)] = sums[half * count : (half + 1) * count]
@@ -441,26 +419,25 @@
     width = sparse_desc.shape[0] * Y * XL
     other_desc = move(env_desc, other_core)
     half = sparse_unit(sparse_desc)
-    from_up, from_down = move(half, up), move(half, down)
+    count = half.shape[0]
+    first = move(half, onward)
     near = move(half, across)
+    second = move(rows_of(half, 0, count, (other_desc,)), back)
+    far = move(first, onward)
+    near_first, near_second = move(first, across), move(second, across)
     *members, inverse, more_owner, pick, pick_more = book(extra_atoms, owner_slots, env_rows)
     envs = env_unit(env_desc, other_desc, (near, inverse))
     sums = jax.ShapeDtypeStruct((HELD_ROWS, 2 * LANES), jnp.float32)
     sums_0 = call(early_call, (), (half, near), envs, members, sums)
-    far = move(choose(from_up, from_down, (sums_0,)), onward)
-    near_up = move(from_up, across)
-    sums_1 = call(early_call, (), (from_up, from_down), envs, members, sums)
-    after = (sums_1,)
-    count = half.shape[0]
-    near_down = move(rows_of(from_down, 0, count, after), across)
+    sums_1 = call(early_call, (), (first, second), envs, members, sums)
     by_y = count // 16 * 3 // 8 * 16
-    near_far_a = move(rows_of(near, 0, by_y, (far, *after)), opposite)
-    near_far_b = move(rows_of(far, by_y, count - by_y, after), across)
-    sums_2 = call(early_call, (), (near_up, far), envs, members, sums)
+    near_far_a = move(rows_of(near, 0, by_y, (far, sums_1)), opposite)
+    near_far_b = move(rows_of(far, by_y, count - by_y, (sums_1,)), across)
+    sums_2 = call(early_call, (), (near_first, far), envs, members, sums)
     codes = call(
         last_call,
         (sums_0, sums_1, sums_2, inverse, more_owner),
-        (near_down, near_far_a, near_far_b),
+        (near_second, near_far_a, near_far_b),
         envs,
         members,
         jax.ShapeDtypeStruct((ROWS // 2, 2 * SENT, LANES), jnp.int16),

time: 69 us -> 66.5 us (0.964)
  blocking collectives: 26.6 us -> 24.9 us
  starting transfers between devices: 10.8 us -> 12.3 us
  local copies, waits for them, and re-layouts: 1.37 us -> 0.01 us
  waiting for transfers between devices: 9.95 us -> 8.84 us
    all_to_all x1, blocking collectives: 26.6 us -> 24.9 us  [on_device(): lax.all_to_all(codes.reshape(ROWS, SENT, LANES), 'rows', 0, 0, tiled=True)]
    ppermute x9, starting transfers between devices: 10.8 us -> 12.3 us  [move(): return lax.ppermute(array, ('sparse', 'rows'), pairs)]
    unnamed x4, local copies, waits for them, and re-layouts: 1.37 us -> 0.01 us
    ppermute x9, waiting for transfers between devices: 9.95 us -> 8.84 us  [move(): return lax.ppermute(array, ('sparse', 'rows'), pairs)]
  transfers between devices with their start and end apart: 9 -> 9, of which waited for: 4 -> 4; matrix products, arithmetic and copies ran while one was open for 0% -> 0% of each run, Pallas kernels for 23% -> 24%
where the time goes in v4:
time: 66.5 us; the launch traced here: 66.1 us
  blocking collectives  24.9 us (37%)
  Pallas kernels  19.9 us (30%)
  starting transfers between devices  12.3 us (18%)
  waiting for transfers between devices  8.84 us (13%)
    all_to_all x1, blocking collectives, on_device(): lax.all_to_all(codes.reshape(ROWS, SENT, LANES), 'rows', 0, 0, tiled=True)  24.9 us
    ppermute x9, starting transfers between devices, move(): return lax.ppermute(array, ('sparse', 'rows'), pairs)  12.3 us
    pallas_call x4, Pallas kernels, call(): pl.pallas_call(kernel, in_specs=[VMEM] * len(operands), out_specs=VMEM, o...  12 us
    ppermute x9, waiting for transfers between devices, move(): return lax.ppermute(array, ('sparse', 'rows'), pairs)  8.84 us
    pallas_call x1, Pallas kernels, env_unit(): pl.pallas_call(env_kernel, in_specs=[ANY] * (2 + len(after)), out_specs=[...  4.24 us
  transfers between devices with their start and end apart: 9, of which 4 were waited for; matrix products, arithmetic and copies ran while one was open for 0% of the time, Pallas kernels for 24%

profile of v4, /device:TPU:6, one launch (start us, length us, event | category | flops | bytes accessed | tf_op | source)
XLA Modules:
  0.0 66.1 jit_solution(6540519616716819100)
XLA Ops:
  0.0 0.0 copy-start
  0.0 0.0 copy-start.1
  0.0 0.0 collective-permute-start.1
  0.0 1.3 %sparse_unit.1.a.array_ref = bf16[128,2048]{1,0:T(8,128)(2,1)S(1)} custom-call(bf16[256,2048]{1,0:T(8,128)(2,1)} %desc_ref.1), custom_call_target="tpu_custom_call" | custom-call | flops 1048576 | bytes 1048576 | tf_op jit(solution)/shard_map/sparse_unit/pallas_call | solution.py:97
  1.3 1.7 %collective-permute-start.2 = (bf16[128,2048]{1,0:T(8,128)(2,1)S(1)}, bf16[128,2048]{1,0:T(8,128)(2,1)S(1)}, u32[]{:S(2)}, u32[]{:S(2)}) collective-permute-start(bf16[128,2048]{1,0:T(8,128)(2,1)S(1)} %sparse_unit.1.a.array_ref), channel_id=1, source_target_pairs={{0,64},{1,193},{2,66},{3,195},{4,68},{5,197},{6,70},{7,199},{8,72}... | collective-permute-start | bytes 1572872 | tf_op jit(solution)/shard_map/ppermute | solution.py:40
  3.0 0.8 %collective-permute-start = (bf16[128,2048]{1,0:T(8,128)(2,1)S(1)}, bf16[128,2048]{1,0:T(8,128)(2,1)S(1)}, u32[]{:S(2)}, u32[]{:S(2)}) collective-permute-start(bf16[128,2048]{1,0:T(8,128)(2,1)S(1)} %sparse_unit.1.a.array_ref), channel_id=1, source_target_pairs={{0,32},{1,35},{2,34},{3,33},{4,36},{5,39},{6,38},{7,37},{8,40},{9,... | collective-permute-start | bytes 1572872 | tf_op jit(solution)/shard_map/ppermute | solution.py:40
  3.8 3.6 %collective-permute-done.1.other_desc.refs_0_ = bf16[1024,2048]{1,0:T(8,128)(2,1)S(1)} collective-permute-done((bf16[1024,2048]{1,0:T(8,128)(2,1)}, bf16[1024,2048]{1,0:T(8,128)(2,1)S(1)}, u32[]{:S(2)}, u32[]{:S(2)}) %collective-permute-start.1) | collective-permute-done | bytes 4194336 | tf_op jit(solution)/shard_map/ppermute | solution.py:40
  7.4 3.1 %collective-permute-start.3 = (bf16[128,2048]{1,0:T(8,128)(2,1)S(1)}, bf16[128,2048]{1,0:T(8,128)(2,1)S(1)}, u32[]{:S(2)}, u32[]{:S(2)}) collective-permute-start(bf16[128,2048]{1,0:T(8,128)(2,1)S(1)} %rows_of.3), channel_id=1, source_target_pairs={{0,192},{1,65},{2,194},{3,67},{4,196},{5,69},{6,198},{7,71},{8,200... | collective-permute-start | bytes 1572872 | tf_op jit(solution)/shard_map/ppermute | solution.py:40
  10.5 1.5 %collective-permute-done.2.a = bf16[128,2048]{1,0:T(8,128)(2,1)S(1)} collective-permute-done((bf16[128,2048]{1,0:T(8,128)(2,1)S(1)}, bf16[128,2048]{1,0:T(8,128)(2,1)S(1)}, u32[]{:S(2)}, u32[]{:S(2)}) %collective-permute-start.2) | collective-permute-done | bytes 524320 | tf_op jit(solution)/shard_map/ppermute | solution.py:40
  12.0 0.4 collective-permute-start.5
  12.4 0.8 %collective-permute-start.4 = (bf16[128,2048]{1,0:T(8,128)(2,1)S(1)}, bf16[128,2048]{1,0:T(8,128)(2,1)S(1)}, u32[]{:S(2)}, u32[]{:S(2)}) collective-permute-start(bf16[128,2048]{1,0:T(8,128)(2,1)S(1)} %collective-permute-done.2.a), channel_id=1, source_target_pairs={{0,32},{1,35},{2,34},{3,33},{4,36},{5,39},{6,38},{7,37},{8,40},{9,... | collective-permute-start | bytes 1572872 | tf_op jit(solution)/shard_map/ppermute | solution.py:40
  13.2 0.0 copy-done
  13.2 0.0 copy-done.1
  13.2 1.1 %book.1 = (bf16[136,1024]{1,0:T(8,128)(2,1)S(1)}, bf16[136,1024]{1,0:T(8,128)(2,1)S(1)}, f32[136,1]{1,0:T(8,128)S(1)}, s32[1,128]{1,0:T(1,128)S(1)}, bf16[64,128...) custom-call(s32[1,1024]{1,0:T(1,128)S(1)} %copy-done, s32[1,1024]{1,0:T(1,128)S(1)} %copy-done.1), custom_call_target="tpu_custom_call" | custom-call | flops 4194304 | bytes 1048576 | tf_op jit(solution)/shard_map/book/pallas_call | solution.py:265
  14.3 0.0 collective-permute-done.refs_0_.b.array_ref
  14.3 4.2 %env_unit.1 = (bf16[1024,2048]{1,0:T(8,128)(2,1)S(1)}, bf16[1024,2048]{1,0:T(8,128)(2,1)S(1)}) custom-call(bf16[1024,2048]{1,0:T(8,128)(2,1)} %own_desc.1, bf16[1024,2048]{1,0:T(8,128)(2,1)S(1)} %collective-permute-done.1.other_desc.refs_0_, bf16[128,2048]{1,0:T(8,128)(2,1)S(1)} %collective-permute-done.refs_0_.b.array_ref, ...), custom_call_target="tpu_custom_call" | custom-call | flops 33554432 | bytes 16777216 | tf_op jit(solution)/shard_map/env_unit/pallas_call | solution.py:133
  18.6 1.5 %collective-permute-done.3.b = bf16[128,2048]{1,0:T(8,128)(2,1)S(1)} collective-permute-done((bf16[128,2048]{1,0:T(8,128)(2,1)S(1)}, bf16[128,2048]{1,0:T(8,128)(2,1)S(1)}, u32[]{:S(2)}, u32[]{:S(2)}) %collective-permute-start.3) | collective-permute-done | bytes 524320 | tf_op jit(solution)/shard_map/ppermute | solution.py:40
  20.1 0.8 %collective-permute-start.6 = (bf16[128,2048]{1,0:T(8,128)(2,1)S(1)}, bf16[128,2048]{1,0:T(8,128)(2,1)S(1)}, u32[]{:S(2)}, u32[]{:S(2)}) collective-permute-start(bf16[128,2048]{1,0:T(8,128)(2,1)S(1)} %collective-permute-done.3.b), channel_id=1, source_target_pairs={{0,32},{1,35},{2,34},{3,33},{4,36},{5,39},{6,38},{7,37},{8,40},{9,... | collective-permute-start | bytes 1572872 | tf_op jit(solution)/shard_map/ppermute | solution.py:40
  20.9 3.0 %early_call.4.refs_1_.refs_0_.sums_1 = f32[136,256]{1,0:T(8,128)S(1)} custom-call(bf16[128,2048]{1,0:T(8,128)(2,1)S(1)} %collective-permute-done.2.a, bf16[128,2048]{1,0:T(8,128)(2,1)S(1)} %collective-permute-done.3.b, bf16[1024,2048]{1,0:T(8,128)(2,1)S(1)} %get-tuple-element.14.own.refs_3_, bf16[1024,2048]{1,0:T(8,128)(2,1)S(1)} %get-tuple-element.15.other.refs_4_, ...), custom_call_target="tpu_custom_call" | custom-call | flops 2147483648 | bytes 8388608 | tf_op jit(solution)/shard_map/early_call/pallas_call | solution.py:360
  23.9 0.0 collective-permute-done.5.b.refs_0_.array_ref
  24.0 1.5 %collective-permute-start.8 = (bf16[80,2048]{1,0:T(8,128)(2,1)S(1)}, bf16[80,2048]{1,0:T(8,128)(2,1)S(1)}, u32[]{:S(2)}, u32[]{:S(2)}) collective-permute-start(bf16[80,2048]{1,0:T(8,128)(2,1)S(1)} %rows_of.5), channel_id=1, source_target_pairs={{0,32},{1,35},{2,34},{3,33},{4,36},{5,39},{6,38},{7,37},{8,40},{9,... | collective-permute-start | bytes 983048 | tf_op jit(solution)/shard_map/ppermute | solution.py:40
  25.4 3.0 %early_call.3.sums_0 = f32[136,256]{1,0:T(8,128)S(1)} custom-call(bf16[128,2048]{1,0:T(8,128)(2,1)S(1)} %sparse_unit.1.a.array_ref, bf16[128,2048]{1,0:T(8,128)(2,1)S(1)} %collective-permute-done.refs_0_.b.array_ref, bf16[1024,2048]{1,0:T(8,128)(2,1)S(1)} %get-tuple-element.14.own.refs_3_, bf16[1024,2048]{1,0:T(8,128)(2,1)S(1)} %get-tuple-element.15.other.refs_4_, ...), custom_call_target="tpu_custom_call" | custom-call | flops 2147483648 | bytes 8388608 | tf_op jit(solution)/shard_map/early_call/pallas_call | solution.py:360
  28.4 3.2 %collective-permute-start.7 = (bf16[48,2048]{1,0:T(8,128)(2,1)S(1)}, bf16[48,2048]{1,0:T(8,128)(2,1)S(1)}, u32[]{:S(2)}, u32[]{:S(2)}) collective-permute-start(bf16[48,2048]{1,0:T(8,128)(2,1)S(1)} %rows_of.4), channel_id=1, source_target_pairs={{0,128},{1,129},{2,130},{3,131},{4,132},{5,133},{6,134},{7,135},{8... | collective-permute-start | bytes 589832 | tf_op jit(solution)/shard_map/ppermute | solution.py:40
  31.6 0.0 collective-permute-done.4.a
  31.6 3.0 %early_call.5.sums_2 = f32[136,256]{1,0:T(8,128)S(1)} custom-call(bf16[128,2048]{1,0:T(8,128)(2,1)S(1)} %collective-permute-done.4.a, bf16[128,2048]{1,0:T(8,128)(2,1)S(1)} %collective-permute-done.5.b.refs_0_.array_ref, bf16[1024,2048]{1,0:T(8,128)(2,1)S(1)} %get-tuple-element.14.own.refs_3_, bf16[1024,2048]{1,0:T(8,128)(2,1)S(1)} %get-tuple-element.15.other.refs_4_, ...), custom_call_target="tpu_custom_call" | custom-call | flops 2147483648 | bytes 8388608 | tf_op jit(solution)/shard_map/early_call/pallas_call | solution.py:360
  34.6 2.2 %collective-permute-done.7.refs_1_ = bf16[48,2048]{1,0:T(8,128)(2,1)S(1)} collective-permute-done((bf16[48,2048]{1,0:T(8,128)(2,1)S(1)}, bf16[48,2048]{1,0:T(8,128)(2,1)S(1)}, u32[]{:S(2)}, u32[]{:S(2)}) %collective-permute-start.7) | collective-permute-done | bytes 196640 | tf_op jit(solution)/shard_map/ppermute | solution.py:40
  36.9 0.0 collective-permute-done.8.refs_2_
  36.9 0.0 collective-permute-done.6.refs_0_
  36.9 3.1 %last_call.1 = s16[16,80,128]{2,1,0:T(8,128)(2,1)S(1)} custom-call(f32[136,256]{1,0:T(8,128)S(1)} %early_call.3.sums_0, f32[136,256]{1,0:T(8,128)S(1)} %early_call.4.refs_1_.refs_0_.sums_1, f32[136,256]{1,0:T(8,128)S(1)} %early_call.5.sums_2, f32[136,1]{1,0:T(8,128)S(1)} %get-tuple-element.13.refs_1_.inverse, s32[1,128]{1,0:T(1,128)S(1)} %get-tuple-element.18.more_owner, ...), custom_call_target="tpu_custom_call" | custom-call | flops 2147483648 | bytes 8388608 | tf_op jit(solution)/shard_map/last_call/pallas_call | solution.py:360
  40.0 24.9 %all_to_all.5 = s16[32,40,128]{2,1,0:T(8,128)(2,1)S(1)} all-to-all(s16[32,40,128]{2,1,0:T(8,128)(2,1)S(1)} %bitcast.2), channel_id=1, replica_groups=mesh['sparse'=8,'rows'=32] {'rows'}, dimensions={0} | all-to-all | bytes 655360 | tf_op jit(solution)/shard_map/all_to_all | solution.py:445
  64.9 1.2 %combine.1 = f32[32,2048]{1,0:T(8,128)} custom-call(s16[16,80,128]{2,1,0:T(8,128)(2,1)S(1)} %bitcast.3, bf16[64,128]{1,0:T(8,128)(2,1)S(1)} %get-tuple-element.19.pick_ref, bf16[256,128]{1,0:T(8,128)(2,1)S(1)} %get-tuple-element.20.pick_more_ref), custom_call_target="tpu_custom_call" | custom-call | tf_op jit(solution)/shard_map/combine/pallas_call | solution.py:407
  (3 shorter events, 0.1 us)
Async XLA Ops:
  0.0 13.2 %copy-start = (s32[1,1024]{1,0:T(1,128)S(1)}, s32[1,1024]{1,0:T(1,128)}, u32[]{:S(2)}) copy-start(s32[1,1024]{1,0:T(1,128)} %extra_ref.1) | copy-start | bytes 12292
  0.0 13.2 %copy-start.1 = (s32[1,1024]{1,0:T(1,128)S(1)}, s32[1,1024]{1,0:T(1,128)}, u32[]{:S(2)}) copy-start(s32[1,1024]{1,0:T(1,128)} %slots_ref.1) | copy-start | bytes 12292
  0.0 7.4 %collective-permute-start.1 = (bf16[1024,2048]{1,0:T(8,128)(2,1)}, bf16[1024,2048]{1,0:T(8,128)(2,1)S(1)}, u32[]{:S(2)}, u32[]{:S(2)}) collective-permute-start(bf16[1024,2048]{1,0:T(8,128)(2,1)} %own_desc.1), channel_id=1, source_target_pairs={{0,1},{1,0},{2,3},{3,2},{4,5},{5,4},{6,7},{7,6},{8,9},{9,8},{10,11... | collective-permute-start | bytes 12582920 | tf_op jit(solution)/shard_map/ppermute | solution.py:40
  1.3 10.7 %collective-permute-start.2 = (bf16[128,2048]{1,0:T(8,128)(2,1)S(1)}, bf16[128,2048]{1,0:T(8,128)(2,1)S(1)}, u32[]{:S(2)}, u32[]{:S(2)}) collective-permute-start(bf16[128,2048]{1,0:T(8,128)(2,1)S(1)} %sparse_unit.1.a.array_ref), channel_id=1, source_target_pairs={{0,64},{1,193},{2,66},{3,195},{4,68},{5,197},{6,70},{7,199},{8,72}... | collective-permute-start | bytes 1572872 | tf_op jit(solution)/shard_map/ppermute | solution.py:40
  3.0 11.4 %collective-permute-start = (bf16[128,2048]{1,0:T(8,128)(2,1)S(1)}, bf16[128,2048]{1,0:T(8,128)(2,1)S(1)}, u32[]{:S(2)}, u32[]{:S(2)}) collective-permute-start(bf16[128,2048]{1,0:T(8,128)(2,1)S(1)} %sparse_unit.1.a.array_ref), channel_id=1, source_target_pairs={{0,32},{1,35},{2,34},{3,33},{4,36},{5,39},{6,38},{7,37},{8,40},{9,... | collective-permute-start | bytes 1572872 | tf_op jit(solution)/shard_map/ppermute | solution.py:40
  7.4 12.7 %collective-permute-start.3 = (bf16[128,2048]{1,0:T(8,128)(2,1)S(1)}, bf16[128,2048]{1,0:T(8,128)(2,1)S(1)}, u32[]{:S(2)}, u32[]{:S(2)}) collective-permute-start(bf16[128,2048]{1,0:T(8,128)(2,1)S(1)} %rows_of.3), channel_id=1, source_target_pairs={{0,192},{1,65},{2,194},{3,67},{4,196},{5,69},{6,198},{7,71},{8,200... | collective-permute-start | bytes 1572872 | tf_op jit(solution)/shard_map/ppermute | solution.py:40
  12.0 11.9 %collective-permute-start.5 = (bf16[128,2048]{1,0:T(8,128)(2,1)S(1)}, bf16[128,2048]{1,0:T(8,128)(2,1)S(1)}, u32[]{:S(2)}, u32[]{:S(2)}) collective-permute-start(bf16[128,2048]{1,0:T(8,128)(2,1)S(1)} %collective-permute-done.2.a), channel_id=1, source_target_pairs={{0,64},{1,193},{2,66},{3,195},{4,68},{5,197},{6,70},{7,199},{8,72}... | collective-permute-start | bytes 1572872 | tf_op jit(solution)/shard_map/ppermute | solution.py:40
  12.4 19.2 %collective-permute-start.4 = (bf16[128,2048]{1,0:T(8,128)(2,1)S(1)}, bf16[128,2048]{1,0:T(8,128)(2,1)S(1)}, u32[]{:S(2)}, u32[]{:S(2)}) collective-permute-start(bf16[128,2048]{1,0:T(8,128)(2,1)S(1)} %collective-permute-done.2.a), channel_id=1, source_target_pairs={{0,32},{1,35},{2,34},{3,33},{4,36},{5,39},{6,38},{7,37},{8,40},{9,... | collective-permute-start | bytes 1572872 | tf_op jit(solution)/shard_map/ppermute | solution.py:40
  20.1 16.8 %collective-permute-start.6 = (bf16[128,2048]{1,0:T(8,128)(2,1)S(1)}, bf16[128,2048]{1,0:T(8,128)(2,1)S(1)}, u32[]{:S(2)}, u32[]{:S(2)}) collective-permute-start(bf16[128,2048]{1,0:T(8,128)(2,1)S(1)} %collective-permute-done.3.b), channel_id=1, source_target_pairs={{0,32},{1,35},{2,34},{3,33},{4,36},{5,39},{6,38},{7,37},{8,40},{9,... | collective-permute-start | bytes 1572872 | tf_op jit(solution)/shard_map/ppermute | solution.py:40
  24.0 12.9 %collective-permute-start.8 = (bf16[80,2048]{1,0:T(8,128)(2,1)S(1)}, bf16[80,2048]{1,0:T(8,128)(2,1)S(1)}, u32[]{:S(2)}, u32[]{:S(2)}) collective-permute-start(bf16[80,2048]{1,0:T(8,128)(2,1)S(1)} %rows_of.5), channel_id=1, source_target_pairs={{0,32},{1,35},{2,34},{3,33},{4,36},{5,39},{6,38},{7,37},{8,40},{9,... | collective-permute-start | bytes 983048 | tf_op jit(solution)/shard_map/ppermute | solution.py:40
  28.4 8.4 %collective-permute-start.7 = (bf16[48,2048]{1,0:T(8,128)(2,1)S(1)}, bf16[48,2048]{1,0:T(8,128)(2,1)S(1)}, u32[]{:S(2)}, u32[]{:S(2)}) collective-permute-start(bf16[48,2048]{1,0:T(8,128)(2,1)S(1)} %rows_of.4), channel_id=1, source_target_pairs={{0,128},{1,129},{2,130},{3,131},{4,132},{5,133},{6,134},{7,135},{8... | collective-permute-start | bytes 589832 | tf_op jit(solution)/shard_map/ppermute | solution.py:40
